TPU v7x, 256 devices: a whole 4x4x8 slice. The times are simulated.
256 devices in a mesh: dom: 32 (over y, z), dir: 8 (over x, core).
Axes of the slice: x: 4, y: 4, z: 8, core: 2. Of those that a mesh axis runs over, the one named last changes fastest.
Arguments:
- incident: bfloat16 [2048, 128, 512], P('dom', 'dir'), may hold values from -6 to 6
- cotangent: bfloat16 [2048, 128, 512], P('dom', 'dir'), may hold values from -6 to 6
- mie: float32 [2048, 512], P('dom'), may hold values from 0.2 to 1
- trans: bfloat16 [12, 512, 512], replicated, may hold values from -0.25 to 0.25
- send_rows: int32 [32, 32, 8], P('dom'), may hold values from 0 to 63, as said below
- partner_slot: int32 [2048, 12], P('dom'), may hold values from -1 to 319, as said below
Outputs:
- amplitude: bfloat16 [2048, 128, 512], P('dom', 'dir')
- gradient: float32 [2048, 512], P('dom', 'dir')
Inputs may be any that keep to these rules, and one draw needn't show every extreme that they name: Within each block send_rows[q, d, :] the rows are distinct; over all d every row of device q appears. `partner_slot`: among the rows of one device, every value from 64 to 319 appears exactly once; values below 64 never name the row's own particle; each device has one or more -1 entries.
All inputs are finite; a program needn't handle non-finite values.
Results may differ from a plain program's by a relative error of at most 0.0045.
Values may be sent and summed in bfloat16 or wider, within the bound.
No kernel may reach another device: no remote copies, remote signals or barrier semaphores. Data moves between devices by JAX's collectives and lax.ppermute only.
A program may use at most 128 MiB of HBM per device.

v0:
```python
import jax
import jax.numpy as jnp
from jax import lax
from jax.sharding import PartitionSpec as P


def scatter_back(adj_amp, trans, partner_slot, slot_total):
    count_p, count_n, coef_width = adj_amp.shape
    flat_adj = adj_amp.reshape(count_p * count_n, coef_width)

    def scatter_one_class(carry_sum, class_item):
        matrix, slot_col = class_item
        products = jnp.einsum("rc,dc->rd", flat_adj, matrix, preferred_element_type=jnp.float32)
        target = jnp.where((slot_col >= 0) & (slot_col < slot_total), slot_col, slot_total)
        return (
            carry_sum.at[target].add(products.reshape(count_p, count_n, coef_width), mode="drop"),
            None,
        )

    empty_sum = jnp.zeros((slot_total, count_n, coef_width), jnp.float32)
    result, _ = lax.scan(scatter_one_class, empty_sum, (trans, partner_slot.T))
    return result


def translate(buffer, trans, partner_slot, incident):
    count_p, count_n, coef_width = incident.shape
    slot_total = buffer.shape[0]
    padded = jnp.concatenate([buffer, jnp.zeros((1, count_n, coef_width), buffer.dtype)], axis=0)

    def translate_one_class(carry_sum, class_item):
        matrix, slot_col = class_item
        target = jnp.where(slot_col >= 0, slot_col, slot_total)
        picked = padded[target].reshape(count_p * count_n, coef_width)
        moved = jnp.dot(picked, matrix, preferred_element_type=jnp.float32)
        return (carry_sum + moved.reshape(count_p, count_n, coef_width), None)

    total_field, _ = lax.scan(
        translate_one_class, incident.astype(jnp.float32), (trans, partner_slot.T)
    )
    return total_field


def body(incident, cotangent, mie, trans, send_rows, partner_slot):
    count_p, count_n, coef_width = incident.shape
    peer_count = lax.axis_size("dom")
    rows_sent = send_rows[0]
    slot_cap = rows_sent.shape[1]
    remote_total = peer_count * slot_cap
    slot_total = count_p + remote_total
    mie_col = mie[:, None, :]
    start_amp = (mie_col * incident.astype(jnp.float32)).astype(jnp.bfloat16)
    adj_amp = (mie_col * cotangent.astype(jnp.float32)).astype(jnp.bfloat16)
    flat_sent = rows_sent.reshape(remote_total)
    outgoing = start_amp[flat_sent].reshape(peer_count, slot_cap, count_n, coef_width)
    arrived = lax.all_to_all(outgoing, "dom", split_axis=0, concat_axis=0, tiled=True)
    gathered = scatter_back(adj_amp, trans, partner_slot, slot_total)
    back_part = gathered[count_p:].reshape(peer_count, slot_cap, count_n, coef_width)
    returned = lax.all_to_all(
        back_part.astype(jnp.bfloat16), "dom", split_axis=0, concat_axis=0, tiled=True
    ).astype(back_part.dtype)
    local_adj = gathered[:count_p]
    incoming = returned.reshape(remote_total, count_n, coef_width)
    buffer = jnp.concatenate(
        [start_amp, arrived.reshape(remote_total, count_n, coef_width)], axis=0
    )
    total_field = translate(buffer, trans, partner_slot, incident)
    amplitude = (mie_col * total_field).astype(jnp.bfloat16)
    adjoint = local_adj.at[flat_sent].add(incoming)
    partial_sum = jnp.sum(
        cotangent.astype(jnp.float32) * total_field + incident.astype(jnp.float32) * adjoint, axis=1
    )
    dirs_total = count_n * lax.axis_size("dir")
    summed = lax.psum(partial_sum, "dir")
    share_width = coef_width // lax.axis_size("dir")
    gradient = (
        lax.dynamic_slice_in_dim(summed, lax.axis_index("dir") * share_width, share_width, 1)
        / dirs_total
    )
    return (amplitude, gradient)


def solution(mesh):
    placed = (
        P("dom", "dir", None),
        P("dom", "dir", None),
        P("dom", None),
        P(),
        P("dom", None, None),
        P("dom", None),
    )
    return jax.shard_map(
        body,
        mesh=mesh,
        in_specs=placed,
        out_specs=(P("dom", "dir", None), P("dom", "dir")),
        check_vma=False,
    )
```

profile of v0, /device:TPU:1, one launch (start us, length us, event | category | flops | bytes accessed | tf_op | source)
XLA Modules:
  0.0 443.5 jit_solution(17827764365315252370)
XLA Ops:
  8.0 3.2 fusion.10
  11.3 2.8 gather_fusion.1
  14.0 12.2 %all-to-all-start = ((bf16[32,8,16,512]{3,2,1,0:T(8,128)(2,1)}), bf16[32,8,16,512]{3,2,1,0:T(8,128)(2,1)}, u32[]{:S(2)}, u32[]{:S(2)}) async-start(bf16[32,8,16,512]{3,2,1,0:T(8,128)(2,1)} %bitcast.52), calls=%async_computation | async-start | bytes 8388608 | tf_op jit(solution)/shard_map/all_to_all | solution.py:55
  26.2 5.3 %broadcast_in_dim.17 = f32[320,16,512]{2,1,0:T(8,128)} broadcast(f32[]{:T(128)} %constant.28.clone.1), dimensions={} | broadcast | bytes 10485764 | tf_op jit(solution)/shard_map/broadcast_in_dim | solution.py:20
  31.5 180.6 %while.21 = (s32[]{:T(128)}, f32[320,16,512]{2,1,0:T(8,128)}, s32[12,64]{1,0:T(8,128)}, bf16[12,512,512]{2,1,0:T(8,128)(2,1)}, bf16[1024,512]{1,0:T(8,128)(2,1)}, /*index=5*/s32[]{:T(128)}) while((s32[]{:T(128)}, f32[320,16,512]{2,1,0:T(8,128)}, s32[12,64]{1,0:T(8,128)}, bf16[12,512,512]{2,1,0:T(8,128)(2,1)}, bf16[1024,512]{1,0:T(8,128)(2,1)}, ...), condition=%wide.region_4.5_spmd, body=%wide.region_2.4_spmd.sunk | while | flops 537395648 | bytes 14157129 | solution.py:21
  31.5 3.4 convolution_bitcast_fusion.2
  35.0 1.9 copy.12
  37.6 9.0 %scatter_fusion = f32[320,16,512]{2,1,0:T(8,128)} fusion(f32[320,16,512]{2,1,0:T(8,128)} %get-tuple-element.169, s32[64]{0:T(128)S(1)} %fusion.24, f32[64,16,512]{2,1,0:T(8,128)S(1)} %bitcast.50), kind=kCustom, calls=%fused_computation.2.clone.1 | custom fusion | flops 524288 | bytes 6291712 | tf_op jit(solution)/shard_map/while/body/eval_jaxpr/scatter-add | solution.py:16
  46.6 3.4 convolution_bitcast_fusion.2
  50.0 1.9 copy.12
  52.6 9.0 %scatter_fusion = f32[320,16,512]{2,1,0:T(8,128)} fusion(f32[320,16,512]{2,1,0:T(8,128)} %get-tuple-element.169, s32[64]{0:T(128)S(1)} %fusion.24, f32[64,16,512]{2,1,0:T(8,128)S(1)} %bitcast.50), kind=kCustom, calls=%fused_computation.2.clone.1 | custom fusion | flops 524288 | bytes 6291712 | tf_op jit(solution)/shard_map/while/body/eval_jaxpr/scatter-add | solution.py:16
  61.6 3.4 convolution_bitcast_fusion.2
  65.0 1.9 copy.12
  67.7 9.0 %scatter_fusion = f32[320,16,512]{2,1,0:T(8,128)} fusion(f32[320,16,512]{2,1,0:T(8,128)} %get-tuple-element.169, s32[64]{0:T(128)S(1)} %fusion.24, f32[64,16,512]{2,1,0:T(8,128)S(1)} %bitcast.50), kind=kCustom, calls=%fused_computation.2.clone.1 | custom fusion | flops 524288 | bytes 6291712 | tf_op jit(solution)/shard_map/while/body/eval_jaxpr/scatter-add | solution.py:16
  76.6 3.4 convolution_bitcast_fusion.2
  80.1 1.9 copy.12
  82.7 9.0 %scatter_fusion = f32[320,16,512]{2,1,0:T(8,128)} fusion(f32[320,16,512]{2,1,0:T(8,128)} %get-tuple-element.169, s32[64]{0:T(128)S(1)} %fusion.24, f32[64,16,512]{2,1,0:T(8,128)S(1)} %bitcast.50), kind=kCustom, calls=%fused_computation.2.clone.1 | custom fusion | flops 524288 | bytes 6291712 | tf_op jit(solution)/shard_map/while/body/eval_jaxpr/scatter-add | solution.py:16
  91.7 3.4 convolution_bitcast_fusion.2
  95.1 1.9 copy.12
  97.7 9.0 %scatter_fusion = f32[320,16,512]{2,1,0:T(8,128)} fusion(f32[320,16,512]{2,1,0:T(8,128)} %get-tuple-element.169, s32[64]{0:T(128)S(1)} %fusion.24, f32[64,16,512]{2,1,0:T(8,128)S(1)} %bitcast.50), kind=kCustom, calls=%fused_computation.2.clone.1 | custom fusion | flops 524288 | bytes 6291712 | tf_op jit(solution)/shard_map/while/body/eval_jaxpr/scatter-add | solution.py:16
  106.7 3.4 convolution_bitcast_fusion.2
  110.2 1.9 copy.12
  112.8 9.1 %scatter_fusion = f32[320,16,512]{2,1,0:T(8,128)} fusion(f32[320,16,512]{2,1,0:T(8,128)} %get-tuple-element.169, s32[64]{0:T(128)S(1)} %fusion.24, f32[64,16,512]{2,1,0:T(8,128)S(1)} %bitcast.50), kind=kCustom, calls=%fused_computation.2.clone.1 | custom fusion | flops 524288 | bytes 6291712 | tf_op jit(solution)/shard_map/while/body/eval_jaxpr/scatter-add | solution.py:16
  121.9 3.4 convolution_bitcast_fusion.2
  125.3 1.9 copy.12
  127.9 9.0 %scatter_fusion = f32[320,16,512]{2,1,0:T(8,128)} fusion(f32[320,16,512]{2,1,0:T(8,128)} %get-tuple-element.169, s32[64]{0:T(128)S(1)} %fusion.24, f32[64,16,512]{2,1,0:T(8,128)S(1)} %bitcast.50), kind=kCustom, calls=%fused_computation.2.clone.1 | custom fusion | flops 524288 | bytes 6291712 | tf_op jit(solution)/shard_map/while/body/eval_jaxpr/scatter-add | solution.py:16
  136.9 3.4 convolution_bitcast_fusion.2
  140.3 1.9 copy.12
  142.9 9.0 %scatter_fusion = f32[320,16,512]{2,1,0:T(8,128)} fusion(f32[320,16,512]{2,1,0:T(8,128)} %get-tuple-element.169, s32[64]{0:T(128)S(1)} %fusion.24, f32[64,16,512]{2,1,0:T(8,128)S(1)} %bitcast.50), kind=kCustom, calls=%fused_computation.2.clone.1 | custom fusion | flops 524288 | bytes 6291712 | tf_op jit(solution)/shard_map/while/body/eval_jaxpr/scatter-add | solution.py:16
  151.9 3.4 convolution_bitcast_fusion.2
  155.3 1.9 copy.12
  158.0 9.0 %scatter_fusion = f32[320,16,512]{2,1,0:T(8,128)} fusion(f32[320,16,512]{2,1,0:T(8,128)} %get-tuple-element.169, s32[64]{0:T(128)S(1)} %fusion.24, f32[64,16,512]{2,1,0:T(8,128)S(1)} %bitcast.50), kind=kCustom, calls=%fused_computation.2.clone.1 | custom fusion | flops 524288 | bytes 6291712 | tf_op jit(solution)/shard_map/while/body/eval_jaxpr/scatter-add | solution.py:16
  167.0 3.4 convolution_bitcast_fusion.2
  170.4 1.9 copy.12
  173.1 9.0 %scatter_fusion = f32[320,16,512]{2,1,0:T(8,128)} fusion(f32[320,16,512]{2,1,0:T(8,128)} %get-tuple-element.169, s32[64]{0:T(128)S(1)} %fusion.24, f32[64,16,512]{2,1,0:T(8,128)S(1)} %bitcast.50), kind=kCustom, calls=%fused_computation.2.clone.1 | custom fusion | flops 524288 | bytes 6291712 | tf_op jit(solution)/shard_map/while/body/eval_jaxpr/scatter-add | solution.py:16
  182.1 3.4 convolution_bitcast_fusion.2
  185.5 1.9 copy.12
  188.1 9.0 %scatter_fusion = f32[320,16,512]{2,1,0:T(8,128)} fusion(f32[320,16,512]{2,1,0:T(8,128)} %get-tuple-element.169, s32[64]{0:T(128)S(1)} %fusion.24, f32[64,16,512]{2,1,0:T(8,128)S(1)} %bitcast.50), kind=kCustom, calls=%fused_computation.2.clone.1 | custom fusion | flops 524288 | bytes 6291712 | tf_op jit(solution)/shard_map/while/body/eval_jaxpr/scatter-add | solution.py:16
  197.1 3.4 convolution_bitcast_fusion.2
  200.5 1.9 copy.12
  203.2 9.0 %scatter_fusion = f32[320,16,512]{2,1,0:T(8,128)} fusion(f32[320,16,512]{2,1,0:T(8,128)} %get-tuple-element.169, s32[64]{0:T(128)S(1)} %fusion.24, f32[64,16,512]{2,1,0:T(8,128)S(1)} %bitcast.50), kind=kCustom, calls=%fused_computation.2.clone.1 | custom fusion | flops 524288 | bytes 6291712 | tf_op jit(solution)/shard_map/while/body/eval_jaxpr/scatter-add | solution.py:16
  212.1 6.1 %slice.15 = bf16[256,16,512]{2,1,0:T(8,128)(2,1)} slice(f32[320,16,512]{2,1,0:T(8,128)} %get-tuple-element.57), slice={[64:320], [0:16], [0:512]} | slice | bytes 8388608 | tf_op jit(solution)/shard_map/slice | solution.py:57
  218.2 10.6 %all-to-all-start.1 = ((bf16[32,8,16,512]{3,2,1,0:T(8,128)(2,1)}), bf16[32,8,16,512]{3,2,1,0:T(8,128)(2,1)}, u32[]{:S(2)}, u32[]{:S(2)}) async-start(bf16[32,8,16,512]{3,2,1,0:T(8,128)(2,1)} %bitcast.51), calls=%async_computation.1 | async-start | bytes 8388608 | tf_op jit(solution)/shard_map/all_to_all | solution.py:58
  228.8 3.2 slice.7
  233.6 6.8 %maximum_maximum_fusion = bf16[321,16,512]{2,1,0:T(8,128)(2,1)} fusion(bf16[256,16,512]{2,1,0:T(8,128)(2,1)} %bitcast.12, bf16[64,16,512]{2,1,0:T(8,128)(2,1)S(1)} %get-tuple-element.81, bf16[321]{0:T(512)(128)(2,1)S(1)} %pad.2.clone), kind=kLoop, calls=%fused_computation.20 | loop fusion | flops 5259264 | bytes 10502786 | tf_op jit(solution)/shard_map/concatenate | solution.py:28
  240.4 67.6 %while.20 = (s32[]{:T(128)}, f32[64,16,512]{2,1,0:T(8,128)S(1)}, s32[12,64]{1,0:T(8,128)}, bf16[321,16,512]{2,1,0:T(8,128)(2,1)}, bf16[12,512,512]{2,1,0:T(8,128)(2,1)}, /*index=5*/s32[]{:T(128)}) while((s32[]{:T(128)}, f32[64,16,512]{2,1,0:T(8,128)S(1)}, s32[12,64]{1,0:T(8,128)}, bf16[321,16,512]{2,1,0:T(8,128)(2,1)}, ...), condition=%wide.region_1.2_spmd, body=%wide.region_0.1_spmd.sunk | while | flops 537396544 | bytes 7870025 | solution.py:37
  241.2 3.1 gather_fusion
  246.8 3.1 gather_fusion
  252.4 3.1 gather_fusion
  258.0 3.1 gather_fusion
  263.7 3.1 gather_fusion
  266.8 1.8 convolution_add_fusion.2
  269.3 3.1 gather_fusion
  274.9 3.1 gather_fusion
  280.6 3.1 gather_fusion
  286.2 3.1 gather_fusion
  291.8 3.1 gather_fusion
  297.5 3.1 gather_fusion
  303.1 3.1 gather_fusion
  308.0 14.7 %all-to-all-done.1 = bf16[32,8,16,512]{3,2,1,0:T(8,128)(2,1)} async-done(((bf16[32,8,16,512]{3,2,1,0:T(8,128)(2,1)}), bf16[32,8,16,512]{3,2,1,0:T(8,128)(2,1)}, u32[]{:S(2)}, u32[]{:S(2)}) %all-to-all-start.1) | async-done | bytes 4194336 | tf_op jit(solution)/shard_map/all_to_all | solution.py:58
  322.7 6.6 %bitcast_convert_fusion = f32[256,16,512]{2,1,0:T(8,128)} fusion(bf16[32,8,16,512]{3,2,1,0:T(8,128)(2,1)} %all-to-all-done.1), kind=kLoop, calls=%fused_computation.21 | loop fusion | flops 2097152 | bytes 12582912 | tf_op jit(solution)/shard_map/reshape | solution.py:62
  329.4 39.3 %scatter_fusion.1 = f32[64,16,512]{2,1,0:T(8,128)} fusion(f32[64,16,512]{2,1,0:T(8,128)} %slice.7, s32[256]{0:T(256)S(1)} %bitcast.54, f32[256,16,512]{2,1,0:T(8,128)} %bitcast_convert_fusion), kind=kCustom, calls=%fused_computation.3 | custom fusion | flops 2097152 | bytes 25166848 | tf_op jit(solution)/shard_map/scatter-add | solution.py:68
  368.7 4.4 fusion.9
  373.1 62.1 %all-reduce.2.cloned.1.call-done = f32[64,512]{1,0:T(8,128)} async-done(((f32[64,512]{1,0:T(8,128)}), f32[64,512]{1,0:T(8,128)}) %all-reduce.2.cloned.1.call-update) | async-done | bytes 131088 | tf_op jit(solution)/shard_map/psum | solution.py:73
  (61 shorter events, 40.5 us)
Async XLA Ops:
  14.0 204.1 %all-to-all-start = ((bf16[32,8,16,512]{3,2,1,0:T(8,128)(2,1)}), bf16[32,8,16,512]{3,2,1,0:T(8,128)(2,1)}, u32[]{:S(2)}, u32[]{:S(2)}) async-start(bf16[32,8,16,512]{3,2,1,0:T(8,128)(2,1)} %bitcast.52), calls=%async_computation | async-start | bytes 8388608 | tf_op jit(solution)/shard_map/all_to_all | solution.py:55
  218.2 104.6 %all-to-all-start.1 = ((bf16[32,8,16,512]{3,2,1,0:T(8,128)(2,1)}), bf16[32,8,16,512]{3,2,1,0:T(8,128)(2,1)}, u32[]{:S(2)}, u32[]{:S(2)}) async-start(bf16[32,8,16,512]{3,2,1,0:T(8,128)(2,1)} %bitcast.51), calls=%async_computation.1 | async-start | bytes 8388608 | tf_op jit(solution)/shard_map/all_to_all | solution.py:58
  228.8 206.5 %all-reduce.2.cloned.1.call-start = ((), (), s32[]{:S(2)}) async-start(), calls=%async_computation.2 | async-start | bytes 262144 | tf_op jit(solution)/shard_map/psum | solution.py:73
  329.4 39.3 %copy-start = (bf16[64,16,512]{2,1,0:T(8,128)(2,1)S(1)}, bf16[64,16,512]{2,1,0:T(8,128)(2,1)}, u32[]{:S(2)}) copy-start(bf16[64,16,512]{2,1,0:T(8,128)(2,1)} %param.10) | copy-start | bytes 3145732
  329.4 39.3 %copy-start.1 = (f32[64,512]{1,0:T(8,128)S(1)}, f32[64,512]{1,0:T(8,128)}, u32[]{:S(2)}) copy-start(f32[64,512]{1,0:T(8,128)} %param.12) | copy-start | bytes 393220
Sparse Core Ops, SparseCore 0:
  373.2 61.9 all-reduce.1
where the time goes:
time: 452 us; the launch traced here: 444 us
  other arithmetic  188 us (42%)
  local copies, waits for them, and re-layouts  78.6 us (17%)
  waiting for transfers between devices  76.9 us (17%)
  matrix products  62.6 us (14%)
  starting transfers between devices  22.8 us (5%)
  between operations  14.1 us (3%)
    scatter-add x12, other arithmetic, scatter_one_class(): carry_sum.at[target]  108 us
    psum x1, waiting for transfers between devices, body(): summed = lax.psum(partial_sum, 'dir')  62.1 us
    dot_general x12, matrix products, scatter_one_class(): jnp.einsum('rc,dc->rd', flat_adj, matrix, preferred_element_type=jnp.floa...  41.1 us
    scatter-add x1, other arithmetic, body(): adjoint = local_adj.at[flat_sent].add(incoming)  39.3 us
    gather x12, local copies, waits for them, and re-layouts, translate_one_class(): picked = padded[target].reshape(count_p * count_n, coef_width)  37.2 us
    dot_general x12, local copies, waits for them, and re-layouts, scatter_one_class(): jnp.einsum('rc,dc->rd', flat_adj, matrix, preferred_element_type=jnp.floa...  23 us
    dot_general x12, matrix products, translate_one_class(): moved = jnp.dot(picked, matrix, preferred_element_type=jnp.float32)  21.5 us
    all_to_all x1, waiting for transfers between devices, body(): lax.all_to_all(back_part.astype(jnp.bfloat16), 'dom', split_axis=0, conca...  14.7 us
  transfers between devices with their start and end apart: 3, of which 2 were waited for; matrix products, arithmetic and copies ran while one was open for 61% of the time, Pallas kernels for 0%

commit v1 on v0

v1 whole, which is shorter than its diff:
```python
import functools

import jax
import jax.numpy as jnp
from jax import lax
from jax.experimental import pallas as pl
from jax.experimental.pallas import tpu as pltpu
from jax.sharding import PartitionSpec as P

CHUNKS = 2
TILE = 8
F32 = jnp.float32
BF16 = jnp.bfloat16
MIB = 1 << 20


def vmem():
    return pl.BlockSpec(memory_space=pltpu.VMEM)


def smem():
    return pl.BlockSpec(memory_space=pltpu.SMEM)


def pack_rows(rows_ref, mie_ref, inc_ref, out_ref):
    def one(i, carry):
        row = rows_ref[i]
        scaled = mie_ref[pl.ds(row, 1), :] * inc_ref[row].astype(F32)
        out_ref[i] = scaled.astype(BF16)
        return carry

    lax.fori_loop(0, out_ref.shape[0], one, 0, unroll=8)


def local_part(
    classes,
    chunk_rows,
    slot_ref,
    inc_ref,
    cot_ref,
    mie_ref,
    trans_ref,
    field_ref,
    back_refs,
    grad_ref,
    order_ref,
    count_ref,
    start_ref,
    adj_ref,
    lhs_ref,
    prod_ref,
    table_ref,
):
    count_p, count_n, width = inc_ref.shape
    chunks = len(back_refs)
    stride = count_p + TILE
    dummy = table_ref.shape[0] - 1

    def prepare(p, carry):
        scale = mie_ref[pl.ds(p, 1), :]
        inc = inc_ref[p].astype(F32)
        start_ref[p] = (scale * inc).astype(BF16)
        at = pl.multiple_of(p * count_n, count_n)
        adj_ref[pl.ds(at, count_n), :] = (scale * cot_ref[p].astype(F32)).astype(BF16)
        field_ref[pl.ds(at, count_n), :] = inc
        return carry

    lax.fori_loop(0, count_p, prepare, 0, unroll=4)
    start_ref[count_p] = jnp.zeros((count_n, width), BF16)

    def clear(t, carry):
        table_ref[t] = jnp.zeros((count_n, width), F32)
        return carry

    lax.fori_loop(0, dummy + 1, clear, 0, unroll=4)

    def one_class(k, carry):
        def pick(p, tallies):
            slot = slot_ref[p * classes + k]
            is_local = (slot >= 0) & (slot < count_p)
            source = jnp.where(is_local, slot, count_p)
            at = pl.multiple_of(p * count_n, count_n)
            lhs_ref[pl.ds(at, count_n), :] = start_ref[source]
            remote = slot - count_p
            fresh = []
            for h in range(chunks):
                tally = tallies[h]
                here = (remote >= h * chunk_rows) & (remote < (h + 1) * chunk_rows)
                order_ref[(h * classes + k) * stride + tally] = (
                    remote - h * chunk_rows
                ) * 128 + p
                fresh.append(tally + here.astype(jnp.int32))
            return tuple(fresh)

        tallies = lax.fori_loop(
            0, count_p, pick, tuple(jnp.int32(0) for _ in range(chunks)), unroll=4
        )
        for h in range(chunks):
            count_ref[h * classes + k] = tallies[h]
            for extra in range(TILE):
                order_ref[(h * classes + k) * stride + tallies[h] + extra] = count_p
        field_ref[...] += jnp.dot(lhs_ref[...], trans_ref[k], preferred_element_type=F32)
        prod_ref[...] = lax.dot_general(
            adj_ref[...],
            trans_ref[k],
            (((1,), (1,)), ((), ())),
            preferred_element_type=F32,
        )

        def spread(p, c):
            slot = slot_ref[p * classes + k]
            target = jnp.where(slot >= 0, slot, dummy)
            at = pl.multiple_of(p * count_n, count_n)
            table_ref[target] += prod_ref[pl.ds(at, count_n), :]
            return c

        lax.fori_loop(0, count_p, spread, 0, unroll=4)
        return carry

    lax.fori_loop(0, classes, one_class, 0)

    def finish(p, carry):
        grad_ref[pl.ds(p, 1), :] = jnp.sum(
            inc_ref[p].astype(F32) * table_ref[p], axis=0, keepdims=True
        )
        return carry

    lax.fori_loop(0, count_p, finish, 0, unroll=4)
    for h in range(chunks):

        def export(i, carry, h=h):
            back_refs[h][i] = table_ref[count_p + h * chunk_rows + i].astype(BF16)
            return carry

        lax.fori_loop(0, chunk_rows, export, 0, unroll=4)


def remote_part(
    classes,
    last,
    order_ref,
    count_ref,
    arrived_ref,
    back_ref,
    field_ref,
    trans_ref,
    *rest,
):
    if last:
        cot_ref, mie_ref, part_ref, amp_ref, grad_ref, term_ref, acc_ref, lhs_ref = rest
    else:
        out_ref, term_ref, acc_ref, lhs_ref = rest
    rows_in, count_n, width = arrived_ref.shape
    total = field_ref.shape[0]
    count_p = total // count_n
    stride = count_p + TILE

    def term(i, carry):
        at = pl.multiple_of(i * 8, 8)
        both = arrived_ref[pl.ds(at, 8)].astype(F32) * back_ref[pl.ds(at, 8)].astype(F32)
        term_ref[pl.ds(at, 8), :] = jnp.sum(both, axis=1)
        return carry

    lax.fori_loop(0, rows_in // 8, term, 0)
    acc_ref[pl.ds(0, total), :] = field_ref[...]

    def one_class(k, carry):
        def one_tile(t, c):
            base = k * stride + t * TILE
            for i in range(TILE):
                source = lax.shift_right_logical(order_ref[base + i], 7)
                lhs_ref[pl.ds(i * count_n, count_n), :] = arrived_ref[source]
            moved = jnp.dot(lhs_ref[...], trans_ref[k], preferred_element_type=F32)
            for i in range(TILE):
                p = order_ref[base + i] & 127
                at = pl.multiple_of(p * count_n, count_n)
                acc_ref[pl.ds(at, count_n), :] += moved[i * count_n : (i + 1) * count_n]
            return c

        tiles = lax.shift_right_logical(count_ref[k] + (TILE - 1), 3)
        lax.fori_loop(0, tiles, one_tile, 0)
        return carry

    lax.fori_loop(0, classes, one_class, 0)
    if not last:
        out_ref[...] = acc_ref[pl.ds(0, total), :]
        return

    def finish(p, carry):
        at = pl.multiple_of(p * count_n, count_n)
        field = acc_ref[pl.ds(at, count_n), :]
        amp_ref[p] = (mie_ref[pl.ds(p, 1), :] * field).astype(BF16)
        grad_ref[pl.ds(p, 1), :] = part_ref[pl.ds(p, 1), :] + jnp.sum(
            cot_ref[p].astype(F32) * field, axis=0, keepdims=True
        )
        return carry

    lax.fori_loop(0, count_p, finish, 0, unroll=4)


def combine(scale, rows_ref, mie_ref, part_ref, *rest):
    term_refs, out_ref, acc_ref = rest[:-2], rest[-2], rest[-1]
    acc_ref[...] = jnp.zeros_like(acc_ref)
    per = term_refs[0].shape[0]
    for h, term_ref in enumerate(term_refs):

        def one(i, carry, h=h, term_ref=term_ref):
            row = rows_ref[h * per + i]
            acc_ref[pl.ds(row, 1), :] += term_ref[pl.ds(i, 1), :]
            return carry

        lax.fori_loop(0, per, one, 0, unroll=8)
    out_ref[...] = (part_ref[...] + acc_ref[...] / mie_ref[...]) * scale


def body(incident, cotangent, mie, trans, send_rows, partner_slot):
    count_p, count_n, width = incident.shape
    classes = trans.shape[0]
    peers = lax.axis_size("dom")
    dirs = lax.axis_size("dir")
    cap = send_rows.shape[2]
    share = cap // CHUNKS
    chunk_rows = peers * share
    remote_rows = peers * cap
    total = count_p * count_n

    rows = send_rows[0].reshape(peers, CHUNKS, share).transpose(1, 0, 2).reshape(CHUNKS, chunk_rows)
    remote = partner_slot - count_p
    moved = (
        count_p
        + ((remote % cap) // share) * chunk_rows
        + (remote // cap) * share
        + remote % share
    )
    slots = jnp.where(remote >= 0, moved, partner_slot).reshape(-1)

    block = jax.ShapeDtypeStruct((chunk_rows, count_n, width), BF16)
    arrived = []
    for h in range(CHUNKS):
        packed = pl.pallas_call(
            pack_rows,
            out_shape=block,
            in_specs=[smem(), vmem(), vmem()],
            out_specs=vmem(),
            compiler_params=pltpu.CompilerParams(vmem_limit_bytes=8 * MIB),
            cost_estimate=pl.CostEstimate(
                flops=chunk_rows * count_n * width, bytes_accessed=6 * MIB, transcendentals=0
            ),
            name="pack_rows",
        )(rows[h], mie, incident)
        got = lax.all_to_all(
            packed.reshape(peers, share, count_n, width), "dom", split_axis=0, concat_axis=0, tiled=True
        )
        arrived.append(got.reshape(chunk_rows, count_n, width))

    stride = count_p + TILE
    field, back, part, order, count = pl.pallas_call(
        functools.partial(local_part, classes, chunk_rows),
        out_shape=(
            jax.ShapeDtypeStruct((total, width), F32),
            [block] * CHUNKS,
            jax.ShapeDtypeStruct((count_p, width), F32),
            jax.ShapeDtypeStruct((CHUNKS * classes * stride,), jnp.int32),
            jax.ShapeDtypeStruct((CHUNKS * classes,), jnp.int32),
        ),
        in_specs=[smem(), vmem(), vmem(), vmem(), vmem()],
        out_specs=(vmem(), [vmem()] * CHUNKS, vmem(), smem(), smem()),
        scratch_shapes=[
            pltpu.VMEM((count_p + 1, count_n, width), BF16),
            pltpu.VMEM((total, width), BF16),
            pltpu.VMEM((total, width), BF16),
            pltpu.VMEM((total, width), F32),
            pltpu.VMEM((count_p + remote_rows + 1, count_n, width), F32),
        ],
        compiler_params=pltpu.CompilerParams(vmem_limit_bytes=44 * MIB),
        cost_estimate=pl.CostEstimate(
            flops=4 * classes * total * width * width, bytes_accessed=20 * MIB, transcendentals=0
        ),
        name="local_part",
    )(slots, incident, cotangent, mie, trans)
    order = order.reshape(CHUNKS, classes * stride)
    count = count.reshape(CHUNKS, classes)

    returned = []
    for h in range(CHUNKS):
        last = h == CHUNKS - 1
        term_shape = jax.ShapeDtypeStruct((chunk_rows, width), F32)
        if last:
            out_shape = (
                jax.ShapeDtypeStruct((count_p, count_n, width), BF16),
                jax.ShapeDtypeStruct((count_p, width), F32),
                term_shape,
            )
            extra = (cotangent, mie, part)
        else:
            out_shape = (jax.ShapeDtypeStruct((total, width), F32), term_shape)
            extra = ()
        results = pl.pallas_call(
            functools.partial(remote_part, classes, last),
            out_shape=out_shape,
            in_specs=[smem(), smem()] + [vmem()] * (4 + len(extra)),
            out_specs=(vmem(),) * len(out_shape),
            scratch_shapes=[
                pltpu.VMEM((total + count_n, width), F32),
                pltpu.VMEM((TILE * count_n, width), BF16),
            ],
            compiler_params=pltpu.CompilerParams(vmem_limit_bytes=28 * MIB),
            cost_estimate=pl.CostEstimate(
                flops=2 * chunk_rows * count_n * width * width, bytes_accessed=14 * MIB, transcendentals=0
            ),
            name="remote_part",
        )(order[h], count[h], arrived[h], back[h], field, trans, *extra)
        if last:
            amplitude, part, term = results
        else:
            field, term = results
        term = lax.all_to_all(
            term.reshape(peers, share, width), "dom", split_axis=0, concat_axis=0, tiled=True
        )
        returned.append(term.reshape(chunk_rows, width))

    mine = pl.pallas_call(
        functools.partial(combine, 1.0 / (count_n * dirs)),
        out_shape=jax.ShapeDtypeStruct((count_p, width), F32),
        in_specs=[smem()] + [vmem()] * (2 + CHUNKS),
        out_specs=vmem(),
        scratch_shapes=[pltpu.VMEM((count_p, width), F32)],
        compiler_params=pltpu.CompilerParams(vmem_limit_bytes=8 * MIB),
        name="combine",
    )(rows.reshape(-1), mie, part, *returned)
    shares = mine.reshape(count_p, dirs, width // dirs).transpose(1, 0, 2)
    shares = lax.all_to_all(shares, "dir", split_axis=0, concat_axis=0, tiled=True)
    return amplitude, jnp.sum(shares, axis=0)


def solution(mesh):
    placed = (
        P("dom", "dir", None),
        P("dom", "dir", None),
        P("dom", None),
        P(),
        P("dom", None, None),
        P("dom", None),
    )
    return jax.shard_map(
        body,
        mesh=mesh,
        in_specs=placed,
        out_specs=(P("dom", "dir", None), P("dom", "dir")),
        check_vma=False,
    )
```

time: 452 us -> 195 us (0.43); the launches traced: 444 us -> 194 us
  other arithmetic: 188 us -> 1.61 us
  matrix products: 62.6 us -> 0 us
  Pallas kernels: 0 us -> 58.8 us
  local copies, waits for them, and re-layouts: 78.6 us -> 19.9 us
  blocking collectives: 0 us -> 13.8 us
  between operations: 14.1 us -> 0.85 us
  waiting for transfers between devices: 76.9 us -> 65.8 us
  starting transfers between devices: 22.8 us -> 33.4 us
    scatter-add x13 -> x0, other arithmetic: 147 us -> none  [the longest x12 108 us: scatter_one_class(): carry_sum.at[target]]
    dot_general x24 -> x0, matrix products: 62.6 us -> none  [the longest x12 41.1 us: scatter_one_class(): jnp.einsum('rc,dc->rd', flat_adj, matrix, preferred_element_type=jnp.floa...]
    psum x1 -> x0, waiting for transfers between devices: 62.1 us -> none  [body(): summed = lax.psum(partial_sum, 'dir')]
    pallas_call x0 -> x6, Pallas kernels: none -> 58.8 us  [the longest x1 35.2 us: body(): pl.pallas_call(functools.partial(local_part, classes, chunk_rows), out_sh...]
    all_to_all x2 -> x4, waiting for transfers between devices: 14.7 us -> 65.8 us  [the longest x2 47.4 us: body(): lax.all_to_all(packed.reshape(peers, share, count_n, width), 'dom', split...]
    gather x13 -> x0, local copies, waits for them, and re-layouts: 40 us -> none  [the longest x12 37.2 us: translate_one_class(): picked = padded[target].reshape(count_p * count_n, coef_width)]
    dot_general x12 -> x0, local copies, waits for them, and re-layouts: 23 us -> none  [scatter_one_class(): jnp.einsum('rc,dc->rd', flat_adj, matrix, preferred_element_type=jnp.floa...]
    select_n x25 -> x1, other arithmetic: 16.8 us -> 0.02 us  [body(): slots = jnp.where(remote >= 0, moved, partner_slot).reshape(-1)]
  transfers between devices with their start and end apart: 3 -> 4, of which waited for: 2 -> 4; matrix products, arithmetic and copies ran while one was open for 61% -> 1% of each run, Pallas kernels for 0% -> 23%
where the time goes in v1:
time: 195 us; the launch traced here: 194 us
  waiting for transfers between devices  65.8 us (34%)
  Pallas kernels  58.8 us (30%)
  starting transfers between devices  33.4 us (17%)
  local copies, waits for them, and re-layouts  19.9 us (10%)
  blocking collectives  13.8 us (7%)
    all_to_all x2, waiting for transfers between devices, body(): lax.all_to_all(packed.reshape(peers, share, count_n, width), 'dom', split...  47.4 us
    pallas_call x1, Pallas kernels, body(): pl.pallas_call(functools.partial(local_part, classes, chunk_rows), out_sh...  35.2 us
    all_to_all x2, starting transfers between devices, body(): lax.all_to_all(packed.reshape(peers, share, count_n, width), 'dom', split...  19.3 us
    all_to_all x2, waiting for transfers between devices, body(): lax.all_to_all(term.reshape(peers, share, width), 'dom', split_axis=0, co...  18.3 us
    pallas_call x2, Pallas kernels, body(): pl.pallas_call(functools.partial(remote_part, classes, last), out_shape=o...  16.9 us
    unnamed x42, local copies, waits for them, and re-layouts  16.1 us
    all_to_all x2, starting transfers between devices, body(): lax.all_to_all(term.reshape(peers, share, width), 'dom', split_axis=0, co...  14.2 us
    all_to_all x1, blocking collectives, body(): lax.all_to_all(shares, 'dir', split_axis=0, concat_axis=0, tiled=True)  13.8 us
  transfers between devices with their start and end apart: 4, of which 4 were waited for; matrix products, arithmetic and copies ran while one was open for 1% of the time, Pallas kernels for 23%

profile of v1, /device:TPU:1, one launch (start us, length us, event | category | flops | bytes accessed | tf_op | source)
XLA Modules:
  0.0 194.1 jit_solution(7287835683391966620)
XLA Ops:
  0.6 0.8 copy.12
  1.4 0.0 copy-start.15
  1.4 0.6 copy-done.15
  2.0 0.1 squeeze.5.rows_ref
  2.1 0.0 copy-start.3
  2.1 1.2 copy-done.3
  3.4 0.0 copy-start.5
  3.4 0.9 copy-done.5
  4.3 2.4 %pack_rows.3 = bf16[128,16,512]{2,1,0:T(8,128)(2,1)} custom-call(s32[128]{0:T(128)S(1)} %squeeze.5.rows_ref, f32[64,512]{1,0:T(8,128)S(1)} %copy-done.5, bf16[64,16,512]{2,1,0:T(8,128)(2,1)S(1)} %copy-done.3), custom_call_target="tpu_custom_call" | custom-call | flops 1048576 | bytes 6291456 | tf_op jit(solution)/shard_map/pack_rows/pallas_call | solution.py:240
  6.7 0.0 copy-start.4
  6.7 12.2 %all-to-all-start.1 = ((bf16[32,4,16,512]{3,2,1,0:T(8,128)(2,1)}), bf16[32,4,16,512]{3,2,1,0:T(8,128)(2,1)S(1)}, u32[]{:S(2)}, u32[]{:S(2)}) async-start(bf16[32,4,16,512]{3,2,1,0:T(8,128)(2,1)} %bitcast.4), calls=%async_computation.1 | async-start | bytes 4194304 | tf_op jit(solution)/shard_map/all_to_all | solution.py:251
  18.8 0.1 squeeze.4.rows_ref
  18.9 0.0 copy-done.4
  18.9 0.0 copy-done.6
  19.0 2.3 %pack_rows.2 = bf16[128,16,512]{2,1,0:T(8,128)(2,1)} custom-call(s32[128]{0:T(128)S(1)} %squeeze.4.rows_ref, f32[64,512]{1,0:T(8,128)S(1)} %copy-done.6, bf16[64,16,512]{2,1,0:T(8,128)(2,1)S(1)} %copy-done.4), custom_call_target="tpu_custom_call" | custom-call | flops 1048576 | bytes 6291456 | tf_op jit(solution)/shard_map/pack_rows/pallas_call | solution.py:240
  21.3 46.4 %all-to-all-done.1 = bf16[32,4,16,512]{3,2,1,0:T(8,128)(2,1)S(1)} async-done(((bf16[32,4,16,512]{3,2,1,0:T(8,128)(2,1)}), bf16[32,4,16,512]{3,2,1,0:T(8,128)(2,1)S(1)}, u32[]{:S(2)}, u32[]{:S(2)}) %all-to-all-start.1) | async-done | bytes 2097184 | tf_op jit(solution)/shard_map/all_to_all | solution.py:251
  67.7 0.0 copy-start.1
  67.7 0.0 copy-start.17
  67.7 1.4 copy-done.1
  69.1 7.1 %all-to-all-start = ((bf16[32,4,16,512]{3,2,1,0:T(8,128)(2,1)}), bf16[32,4,16,512]{3,2,1,0:T(8,128)(2,1)}, u32[]{:S(2)}, u32[]{:S(2)}) async-start(bf16[32,4,16,512]{3,2,1,0:T(8,128)(2,1)} %bitcast.2), calls=%async_computation | async-start | bytes 4194304 | tf_op jit(solution)/shard_map/all_to_all | solution.py:251
  76.3 0.0 copy-done.17
  76.3 0.1 copy.11
  76.4 0.1 reshape.49.slot_ref
  76.5 0.0 copy-start.11
  76.5 1.3 copy-done.11
  77.9 35.2 %local_part.1 = (f32[1024,512]{1,0:T(8,128)S(1)}, bf16[128,16,512]{2,1,0:T(8,128)(2,1)S(1)}, bf16[128,16,512]{2,1,0:T(8,128)(2,1)S(1)}, f32[64,512]{1,0:T(8,128)S(1)}, s32[1728]{0:T(1024)S(1)}, /*index=5*/s32[24]{0:T(128)S(1)}) custom-call(s32[768]{0:T(1024)S(1)} %reshape.49.slot_ref, bf16[64,16,512]{2,1,0:T(8,128)(2,1)S(1)} %copy-done.4, ...), custom_call_target="tpu_custom_call" | custom-call | flops 12884901888 | bytes 20971520 | tf_op jit(solution)/shard_map/local_part/pallas_call | solution.py:257
  113.1 0.0 copy-start.7
  113.1 1.4 copy-done.7
  114.5 0.7 copy-done.13
  115.1 0.1 fusion.13
  115.2 0.1 fusion.12
  115.3 0.0 slice-done
  115.3 0.0 slice-done.1
  115.3 0.0 copy-done.2
  115.3 0.0 copy-start.12
  115.3 7.2 %remote_part.2 = (f32[1024,512]{1,0:T(8,128)S(1)}, f32[128,512]{1,0:T(8,128)S(1)}) custom-call(s32[864]{0:T(1024)S(1)} %get-tuple-element.26.order_ref, s32[12]{0:T(128)S(1)} %get-tuple-element.28.count_ref, bf16[128,16,512]{2,1,0:T(8,128)(2,1)S(1)} %bitcast.11, bf16[128,16,512]{2,1,0:T(8,128)(2,1)S(1)} %get-tuple-element.16.back_ref, ...), custom_call_target="tpu_custom_call" | custom-call | flops 1073741824 | bytes 14680064 | tf_op jit(solution)/shard_map/remote_part/pallas_call | solution.py:298
  122.5 0.0 copy-start.9
  122.5 1.4 copy-done.9
  123.9 1.0 all-to-all-done
  124.9 0.0 copy-done.12
  124.9 2.8 %copy-done = bf16[12,512,512]{2,1,0:T(8,128)(2,1)S(1)} copy-done((bf16[12,512,512]{2,1,0:T(8,128)(2,1)S(1)}, bf16[12,512,512]{2,1,0:T(8,128)(2,1)}, u32[]{:S(2)}) %copy-start) | copy-done | bytes 6291480
  127.7 1.6 copy-done.8
  129.3 1.6 copy-done.10
  130.9 0.9 copy-done.14
  131.8 9.7 %remote_part.3 = (bf16[64,16,512]{2,1,0:T(8,128)(2,1)}, f32[64,512]{1,0:T(8,128)S(1)}, f32[128,512]{1,0:T(8,128)S(1)}) custom-call(s32[864]{0:T(1024)S(1)} %get-tuple-element.27.order_ref, s32[12]{0:T(128)S(1)} %get-tuple-element.29.count_ref, bf16[128,16,512]{2,1,0:T(8,128)(2,1)} %bitcast.3.arrived_ref, bf16[128,16,512]{2,1,0:T(8,128)(2,1)S(1)} %copy-done.8, ...), custom_call_target="tpu_custom_call" | custom-call | flops 1073741824 | bytes 14680064 | tf_op jit(solution)/shard_map/remote_part/pallas_call | solution.py:298
  141.5 0.8 reshape.56
  142.3 8.4 %all-to-all-start.3 = ((f32[32,4,512]{2,1,0:T(4,128)}), f32[32,4,512]{2,1,0:T(4,128)S(1)}, u32[]{:S(2)}, u32[]{:S(2)}) async-start(f32[32,4,512]{2,1,0:T(4,128)} %reshape.56), calls=%async_computation.3 | async-start | bytes 524288 | tf_op jit(solution)/shard_map/all_to_all | solution.py:317
  150.7 0.8 reshape.54
  151.5 8.9 %all-to-all-done.3 = f32[32,4,512]{2,1,0:T(4,128)S(1)} async-done(((f32[32,4,512]{2,1,0:T(4,128)}), f32[32,4,512]{2,1,0:T(4,128)S(1)}, u32[]{:S(2)}, u32[]{:S(2)}) %all-to-all-start.3) | async-done | bytes 262176 | tf_op jit(solution)/shard_map/all_to_all | solution.py:317
  160.4 5.7 %all-to-all-start.2 = ((f32[32,4,512]{2,1,0:T(4,128)}), f32[32,4,512]{2,1,0:T(4,128)S(1)}, u32[]{:S(2)}, u32[]{:S(2)}) async-start(f32[32,4,512]{2,1,0:T(4,128)} %reshape.54), calls=%async_computation.2 | async-start | bytes 524288 | tf_op jit(solution)/shard_map/all_to_all | solution.py:317
  166.1 0.0 copy-done.16
  166.1 0.1 reshape_reshape.3.rows_ref
  166.2 0.1 reshape.57.rest_1_
  166.3 9.4 %all-to-all-done.2 = f32[32,4,512]{2,1,0:T(4,128)S(1)} async-done(((f32[32,4,512]{2,1,0:T(4,128)}), f32[32,4,512]{2,1,0:T(4,128)S(1)}, u32[]{:S(2)}, u32[]{:S(2)}) %all-to-all-start.2) | async-done | bytes 262176 | tf_op jit(solution)/shard_map/all_to_all | solution.py:317
  175.8 0.1 reshape.55.rest_0_
  175.9 1.9 combine.1
  177.8 0.1 reshape.58
  177.9 0.1 copy.15
  177.9 0.2 reshape.59
  178.1 13.8 %all_to_all.25 = f32[8,1,4096]{2,1,0:T(1,128)S(1)} all-to-all(f32[8,1,4096]{2,1,0:T(1,128)S(1)} %reshape.59), channel_id=1, replica_groups=mesh['dom'=32,'dir'=8] {'dir'}, dimensions={0} | all-to-all | bytes 262144 | tf_op jit(solution)/shard_map/all_to_all | solution.py:332
  191.9 0.5 broadcast.27
  192.4 1.0 reduce
  193.3 0.1 reshape.60
  193.4 0.6 reduce_sum.9
  (13 shorter events, 0.0 us)
Async XLA Ops:
  1.4 0.6 copy-start.15
  2.1 1.2 copy-start.3
  3.4 0.9 copy-start.5
  6.7 12.3 %copy-start.4 = (bf16[64,16,512]{2,1,0:T(8,128)(2,1)S(1)}, bf16[64,16,512]{2,1,0:T(8,128)(2,1)}, u32[]{:S(2)}) copy-start(bf16[64,16,512]{2,1,0:T(8,128)(2,1)} %inc_ref.5) | copy-start | bytes 3145732
  6.7 12.3 %copy-start.6 = (f32[64,512]{1,0:T(8,128)S(1)}, f32[64,512]{1,0:T(8,128)}, u32[]{:S(2)}) copy-start(f32[64,512]{1,0:T(8,128)} %mie_ref.7) | copy-start | bytes 393220
  6.7 61.1 %all-to-all-start.1 = ((bf16[32,4,16,512]{3,2,1,0:T(8,128)(2,1)}), bf16[32,4,16,512]{3,2,1,0:T(8,128)(2,1)S(1)}, u32[]{:S(2)}, u32[]{:S(2)}) async-start(bf16[32,4,16,512]{3,2,1,0:T(8,128)(2,1)} %bitcast.4), calls=%async_computation.1 | async-start | bytes 4194304 | tf_op jit(solution)/shard_map/all_to_all | solution.py:251
  67.7 1.4 copy-start.1
  67.7 8.5 %copy-start.17 = (s32[64,12]{0,1:T(8,128)S(1)}, s32[64,12]{0,1:T(8,128)}, u32[]{:S(2)}) copy-start(s32[64,12]{0,1:T(8,128)} %param.11) | copy-start | bytes 9220
  69.1 55.8 %all-to-all-start = ((bf16[32,4,16,512]{3,2,1,0:T(8,128)(2,1)}), bf16[32,4,16,512]{3,2,1,0:T(8,128)(2,1)}, u32[]{:S(2)}, u32[]{:S(2)}) async-start(bf16[32,4,16,512]{3,2,1,0:T(8,128)(2,1)} %bitcast.2), calls=%async_computation | async-start | bytes 4194304 | tf_op jit(solution)/shard_map/all_to_all | solution.py:251
  76.4 38.9 %slice-start = ((s8[6291456]{0:T(1024)(128)(4,1)}), s8[2097152]{0:T(1024)(128)(4,1)S(1)}, s32[]{:S(2)}) async-start(s8[6291456]{0:T(1024)(128)(4,1)} %bitcast.9), calls=%async_computation.5 | async-start | bytes 4194304
  76.5 1.4 copy-start.11
  77.9 37.4 %slice-start.1 = ((s8[6291456]{0:T(1024)(128)(4,1)}), s8[4194304]{0:T(1024)(128)(4,1)S(1)}, s32[]{:S(2)}) async-start(s8[6291456]{0:T(1024)(128)(4,1)} %bitcast.9), calls=%async_computation.6 | async-start | bytes 8388608
  77.9 37.4 %copy-start.2 = (bf16[32,4,16,512]{3,2,1,0:T(8,128)(2,1)S(1)}, bf16[32,4,16,512]{3,2,1,0:T(8,128)(2,1)}, u32[]{:S(2)}) copy-start(bf16[32,4,16,512]{3,2,1,0:T(8,128)(2,1)} %copy-done.1) | copy-start | bytes 6291460
  113.1 1.4 copy-start.7
  114.5 0.7 copy-start.13
  115.3 9.6 %copy-start.12 = (bf16[64,16,512]{2,1,0:T(8,128)(2,1)S(1)}, bf16[64,16,512]{2,1,0:T(8,128)(2,1)}, u32[]{:S(2)}) copy-start(bf16[64,16,512]{2,1,0:T(8,128)(2,1)} %rest_0_.1) | copy-start | bytes 3145732
  122.5 1.4 copy-start.9
  124.9 2.8 %copy-start = (bf16[12,512,512]{2,1,0:T(8,128)(2,1)S(1)}, bf16[12,512,512]{2,1,0:T(8,128)(2,1)}, u32[]{:S(2)}) copy-start(bf16[12,512,512]{2,1,0:T(8,128)(2,1)} %trans_ref.5) | copy-start | bytes 18874372
  127.7 1.6 copy-start.8
  129.3 1.6 copy-start.10
  130.9 0.9 copy-start.14
  141.5 24.6 %copy-start.16 = (s32[32,2,4]{2,0,1:T(8,128)S(1)}, s32[32,2,4]{2,0,1:T(8,128)}, u32[]{:S(2)}) copy-start(s32[32,2,4]{2,0,1:T(8,128)} %copy-done.15) | copy-start | bytes 3076
  142.3 18.1 %all-to-all-start.3 = ((f32[32,4,512]{2,1,0:T(4,128)}), f32[32,4,512]{2,1,0:T(4,128)S(1)}, u32[]{:S(2)}, u32[]{:S(2)}) async-start(f32[32,4,512]{2,1,0:T(4,128)} %reshape.56), calls=%async_computation.3 | async-start | bytes 524288 | tf_op jit(solution)/shard_map/all_to_all | solution.py:317
  160.4 15.4 %all-to-all-start.2 = ((f32[32,4,512]{2,1,0:T(4,128)}), f32[32,4,512]{2,1,0:T(4,128)S(1)}, u32[]{:S(2)}, u32[]{:S(2)}) async-start(f32[32,4,512]{2,1,0:T(4,128)} %reshape.54), calls=%async_computation.2 | async-start | bytes 524288 | tf_op jit(solution)/shard_map/all_to_all | solution.py:317

commit v2 on v1

v2 whole, which is shorter than its diff:
```python
import functools

import jax
import jax.numpy as jnp
from jax import lax
from jax.experimental import pallas as pl
from jax.experimental.pallas import tpu as pltpu
from jax.sharding import PartitionSpec as P

SPLITS = (0, 6, 8)
TILE = 8
F32 = jnp.float32
BF16 = jnp.bfloat16
MIB = 1 << 20


def vmem():
    return pl.BlockSpec(memory_space=pltpu.VMEM)


def smem():
    return pl.BlockSpec(memory_space=pltpu.SMEM)


def hbm():
    return pl.BlockSpec(memory_space=pl.ANY)


def pack_rows(low, rows_ref, mie_hbm, inc_hbm, out_hbm, mie_ref, inc_ref, out_ref, in_sem, out_sem):
    parts, part_peers, width = out_sem.shape[0], out_ref.shape[0] // out_sem.shape[0], out_ref.shape[1]
    get_mie = pltpu.make_async_copy(mie_hbm, mie_ref, in_sem.at[0])
    get_inc = pltpu.make_async_copy(inc_hbm, inc_ref, in_sem.at[1])
    get_mie.start()
    get_inc.start()
    get_mie.wait()
    get_inc.wait()

    def put(part):
        here = pl.ds(part * part_peers, part_peers)
        return pltpu.make_async_copy(out_ref.at[here], out_hbm.at[here], out_sem.at[part])

    for part in range(parts):

        def one(i, carry, part=part):
            peer = part * part_peers + i
            for c in range(width):
                row = rows_ref[low + c, peer]
                scaled = mie_ref[pl.ds(row, 1), :] * inc_ref[row].astype(F32)
                out_ref[peer, c] = scaled.astype(BF16)
            return carry

        lax.fori_loop(0, part_peers, one, 0, unroll=2)
        put(part).start()
    for part in range(parts):
        put(part).wait()


def local_part(
    cap,
    slot_ref,
    inc_ref,
    cot_ref,
    mie_ref,
    trans_ref,
    field_ref,
    back_ref,
    grad_ref,
    order_ref,
    count_ref,
    start_ref,
    adj_ref,
    lhs_ref,
    prod_ref,
    adjoint_ref,
):
    count_p, count_n, width = inc_ref.shape
    classes = slot_ref.shape[0]
    chunks = len(SPLITS) - 1
    stride = count_p + TILE
    dummy = back_ref.shape[0] - 1

    def prepare(p, carry):
        scale = mie_ref[pl.ds(p, 1), :]
        inc = inc_ref[p].astype(F32)
        start_ref[p] = (scale * inc).astype(BF16)
        at = pl.multiple_of(p * count_n, count_n)
        adj_ref[pl.ds(at, count_n), :] = (scale * cot_ref[p].astype(F32)).astype(BF16)
        field_ref[pl.ds(at, count_n), :] = inc
        adjoint_ref[p] = jnp.zeros((count_n, width), F32)
        return carry

    lax.fori_loop(0, count_p, prepare, 0, unroll=4)
    start_ref[count_p] = jnp.zeros((count_n, width), BF16)
    adjoint_ref[count_p] = jnp.zeros((count_n, width), F32)

    def one_class(k, carry):
        def pick(p, tallies):
            slot = slot_ref[k, p]
            is_local = (slot >= 0) & (slot < count_p)
            source = jnp.where(is_local, slot, count_p)
            at = pl.multiple_of(p * count_n, count_n)
            lhs_ref[pl.ds(at, count_n), :] = start_ref[source]
            remote = slot - count_p
            peer = lax.div(remote, cap)
            place = remote - peer * cap
            fresh = []
            for h in range(chunks):
                low, high = SPLITS[h], SPLITS[h + 1]
                here = (remote >= 0) & (place >= low) & (place < high)
                index = peer * (high - low) + place - low
                order_ref[(h * classes + k) * stride + tallies[h]] = index * 128 + p
                fresh.append(tallies[h] + here.astype(jnp.int32))
            return tuple(fresh)

        tallies = lax.fori_loop(
            0, count_p, pick, tuple(jnp.int32(0) for _ in range(chunks)), unroll=4
        )
        for h in range(chunks):
            count_ref[h * classes + k] = tallies[h]
            for extra in range(TILE):
                order_ref[(h * classes + k) * stride + tallies[h] + extra] = count_p
        field_ref[...] += jnp.dot(lhs_ref[...], trans_ref[k], preferred_element_type=F32)
        prod_ref[...] = lax.dot_general(
            adj_ref[...],
            trans_ref[k],
            (((1,), (1,)), ((), ())),
            preferred_element_type=F32,
        )

        def spread(p, c):
            slot = slot_ref[k, p]
            is_local = (slot >= 0) & (slot < count_p)
            at = pl.multiple_of(p * count_n, count_n)
            prod = prod_ref[pl.ds(at, count_n), :]
            back_ref[jnp.where(slot >= count_p, slot - count_p, dummy)] = prod.astype(BF16)
            adjoint_ref[jnp.where(is_local, slot, count_p)] += prod
            return c

        lax.fori_loop(0, count_p, spread, 0, unroll=4)
        return carry

    lax.fori_loop(0, classes, one_class, 0)

    def finish(p, carry):
        grad_ref[pl.ds(p, 1), :] = jnp.sum(
            inc_ref[p].astype(F32) * adjoint_ref[p], axis=0, keepdims=True
        )
        return carry

    lax.fori_loop(0, count_p, finish, 0, unroll=4)


def remote_part(
    classes,
    h,
    cap,
    order_ref,
    count_ref,
    arrived_ref,
    back_ref,
    field_ref,
    trans_ref,
    *rest,
):
    last = h == len(SPLITS) - 2
    if last:
        cot_ref, mie_ref, part_ref, before_ref, amp_ref, grad_ref, term_ref, acc_ref, lhs_ref = rest
        term_ref[...] = before_ref[...]
    else:
        out_ref, term_ref, acc_ref, lhs_ref = rest
    low, high = SPLITS[h], SPLITS[h + 1]
    rows_in, count_n, width = arrived_ref.shape
    peers, share = rows_in // (high - low), high - low
    total = field_ref.shape[0]
    count_p = total // count_n
    stride = count_p + TILE
    first = h * classes

    def term(q, carry):
        got = arrived_ref[pl.ds(q * share, share)].astype(F32)
        kept = back_ref[pl.ds(q * cap + low, share)].astype(F32)
        term_ref[q, low:high] = jnp.sum(got * kept, axis=1)
        return carry

    lax.fori_loop(0, peers, term, 0)
    acc_ref[pl.ds(0, total), :] = field_ref[...]

    def one_class(k, carry):
        def one_tile(t, c):
            base = (first + k) * stride + t * TILE
            for i in range(TILE):
                source = lax.shift_right_logical(order_ref[base + i], 7)
                lhs_ref[pl.ds(i * count_n, count_n), :] = arrived_ref[source]
            moved = jnp.dot(lhs_ref[...], trans_ref[k], preferred_element_type=F32)
            for i in range(TILE):
                p = order_ref[base + i] & 127
                at = pl.multiple_of(p * count_n, count_n)
                acc_ref[pl.ds(at, count_n), :] += moved[i * count_n : (i + 1) * count_n]
            return c

        tiles = lax.shift_right_logical(count_ref[first + k] + (TILE - 1), 3)
        lax.fori_loop(0, tiles, one_tile, 0)
        return carry

    lax.fori_loop(0, classes, one_class, 0)
    if not last:
        out_ref[...] = acc_ref[pl.ds(0, total), :]
        return

    def finish(p, carry):
        at = pl.multiple_of(p * count_n, count_n)
        field = acc_ref[pl.ds(at, count_n), :]
        amp_ref[p] = (mie_ref[pl.ds(p, 1), :] * field).astype(BF16)
        grad_ref[pl.ds(p, 1), :] = part_ref[pl.ds(p, 1), :] + jnp.sum(
            cot_ref[p].astype(F32) * field, axis=0, keepdims=True
        )
        return carry

    lax.fori_loop(0, count_p, finish, 0, unroll=4)


def combine(scale, rows_ref, mie_ref, part_ref, term_ref, out_ref, acc_ref):
    acc_ref[...] = jnp.zeros_like(acc_ref)

    def one(q, carry):
        for c in range(term_ref.shape[1]):
            row = rows_ref[c, q]
            acc_ref[pl.ds(row, 1), :] += term_ref[q, pl.ds(c, 1), :]
        return carry

    lax.fori_loop(0, term_ref.shape[0], one, 0)
    whole = (part_ref[...] + acc_ref[...] / mie_ref[...]) * scale
    dirs, half, pair = out_ref.shape
    share = pair // 2
    for r in range(dirs):
        block = whole[:, r * share : (r + 1) * share]
        out_ref[r] = jnp.concatenate([block[:half], block[half:]], axis=1)


def add_shares(in_ref, out_ref):
    summed = jnp.sum(in_ref[...], axis=0)
    share = summed.shape[1] // 2
    out_ref[...] = jnp.concatenate([summed[:, :share], summed[:, share:]], axis=0)


def params(mib):
    return pltpu.CompilerParams(vmem_limit_bytes=mib * MIB)


def cost(flops, mib):
    return pl.CostEstimate(flops=int(flops), bytes_accessed=mib * MIB, transcendentals=0)


def body(incident, cotangent, mie, trans, send_rows, partner_slot):
    count_p, count_n, width = incident.shape
    classes = trans.shape[0]
    peers = lax.axis_size("dom")
    dirs = lax.axis_size("dir")
    cap = send_rows.shape[2]
    remote_rows = peers * cap
    total = count_p * count_n
    chunks = len(SPLITS) - 1
    row_ops = count_p * count_n * width

    rows = jnp.transpose(send_rows[0])
    slots = jnp.transpose(partner_slot)

    def pack(h):
        share = SPLITS[h + 1] - SPLITS[h]
        block = (peers, share, count_n, width)
        return pl.pallas_call(
            functools.partial(pack_rows, SPLITS[h]),
            out_shape=jax.ShapeDtypeStruct(block, BF16),
            in_specs=[smem(), hbm(), hbm()],
            out_specs=hbm(),
            scratch_shapes=[
                pltpu.VMEM((count_p, width), F32),
                pltpu.VMEM((count_p, count_n, width), BF16),
                pltpu.VMEM(block, BF16),
                pltpu.SemaphoreType.DMA((2,)),
                pltpu.SemaphoreType.DMA((4,)),
            ],
            compiler_params=params(8),
            cost_estimate=cost(row_ops, 4),
            name="pack_rows",
        )(rows, mie, incident)

    def send(x):
        return lax.all_to_all(x, "dom", split_axis=0, concat_axis=0, tiled=True)

    stride = count_p + TILE
    field, back, part, order, count = pl.pallas_call(
        functools.partial(local_part, cap),
        out_shape=(
            jax.ShapeDtypeStruct((total, width), F32),
            jax.ShapeDtypeStruct((remote_rows + 1, count_n, width), BF16),
            jax.ShapeDtypeStruct((count_p, width), F32),
            jax.ShapeDtypeStruct((chunks * classes * stride,), jnp.int32),
            jax.ShapeDtypeStruct((chunks * classes,), jnp.int32),
        ),
        in_specs=[smem(), vmem(), vmem(), vmem(), vmem()],
        out_specs=(vmem(), vmem(), vmem(), smem(), smem()),
        scratch_shapes=[
            pltpu.VMEM((count_p + 1, count_n, width), BF16),
            pltpu.VMEM((total, width), BF16),
            pltpu.VMEM((total, width), BF16),
            pltpu.VMEM((total, width), F32),
            pltpu.VMEM((count_p + 1, count_n, width), F32),
        ],
        compiler_params=params(26),
        cost_estimate=cost(4 * classes * row_ops * width, 16),
        name="local_part",
    )(slots, incident, cotangent, mie, trans)

    term = None
    for h in range(chunks):
        last = h == chunks - 1
        share = SPLITS[h + 1] - SPLITS[h]
        packed = pack(h)
        if h > 0:
            packed, part = lax.optimization_barrier((packed, part))
        arrived = send(packed).reshape(peers * share, count_n, width)
        term_shape = jax.ShapeDtypeStruct((peers, cap, width), F32)
        if last:
            out_shape = (
                jax.ShapeDtypeStruct((count_p, count_n, width), BF16),
                jax.ShapeDtypeStruct((count_p, width), F32),
                term_shape,
            )
            extra = (cotangent, mie, part, term)
        else:
            out_shape = (jax.ShapeDtypeStruct((total, width), F32), term_shape)
            extra = ()
        results = pl.pallas_call(
            functools.partial(remote_part, classes, h, cap),
            out_shape=out_shape,
            in_specs=[smem(), smem()] + [vmem()] * (4 + len(extra)),
            out_specs=(vmem(),) * len(out_shape),
            scratch_shapes=[
                pltpu.VMEM((total + count_n, width), F32),
                pltpu.VMEM((TILE * count_n, width), BF16),
            ],
            compiler_params=params(24),
            cost_estimate=cost(2 * peers * share * count_n * width * width, 14),
            name="remote_part",
        )(order, count, arrived, back, field, trans, *extra)
        if last:
            amplitude, part, term = results
        else:
            field, term = results

    term = send(term)
    mine = pl.pallas_call(
        functools.partial(combine, 1.0 / (count_n * dirs)),
        out_shape=jax.ShapeDtypeStruct((dirs, count_p // 2, 2 * width // dirs), F32),
        in_specs=[smem()] + [vmem()] * 3,
        out_specs=vmem(),
        scratch_shapes=[pltpu.VMEM((count_p, width), F32)],
        compiler_params=params(8),
        cost_estimate=cost(row_ops, 1),
        name="combine",
    )(rows, mie, part, term)
    shares = lax.all_to_all(mine, "dir", split_axis=0, concat_axis=0, tiled=True)
    gradient = pl.pallas_call(
        add_shares,
        out_shape=jax.ShapeDtypeStruct((count_p, width // dirs), F32),
        in_specs=[vmem()],
        out_specs=vmem(),
        compiler_params=params(8),
        cost_estimate=cost(row_ops, 1),
        name="add_shares",
    )(shares)
    return amplitude, gradient


def solution(mesh):
    placed = (
        P("dom", "dir", None),
        P("dom", "dir", None),
        P("dom", None),
        P(),
        P("dom", None, None),
        P("dom", None),
    )
    return jax.shard_map(
        body,
        mesh=mesh,
        in_specs=placed,
        out_specs=(P("dom", "dir", None), P("dom", "dir")),
        check_vma=False,
    )
```

time: 195 us -> 180 us (0.923)
  waiting for transfers between devices: 65.8 us -> 26.9 us
  blocking collectives: 13.8 us -> 35.8 us
  local copies, waits for them, and re-layouts: 19.9 us -> 32.8 us
  starting transfers between devices: 33.4 us -> 21.1 us
  Pallas kernels: 58.8 us -> 61.2 us
    all_to_all x4 -> x2, waiting for transfers between devices: 65.8 us -> 26.9 us  [send(): return lax.all_to_all(x, 'dom', split_axis=0, concat_axis=0, tiled=True)]
    all_to_all x1 -> x2, blocking collectives: 13.8 us -> 35.8 us  [the longest x1 22.4 us: send(): return lax.all_to_all(x, 'dom', split_axis=0, concat_axis=0, tiled=True)]
    unnamed x42 -> x48, local copies, waits for them, and re-layouts: 16.1 us -> 32.8 us
    all_to_all x4 -> x2, starting transfers between devices: 33.4 us -> 21.1 us  [send(): return lax.all_to_all(x, 'dom', split_axis=0, concat_axis=0, tiled=True)]
    pallas_call x5 -> x6, Pallas kernels: 56.9 us -> 59.4 us  [the longest x1 38.5 us: body(): pl.pallas_call(functools.partial(local_part, cap), out_shape=(jax.ShapeDt...]
    reshape x7 -> x0, local copies, waits for them, and re-layouts: 2 us -> none  [the longest x2 1.57 us: body(): term.reshape(peers, share, width)]
  transfers between devices with their start and end apart: 4 -> 2, of which waited for: 4 -> 2; matrix products, arithmetic and copies ran while one was open for 1% -> 0% of each run, Pallas kernels for 23% -> 28%
where the time goes in v2:
time: 180 us; the launch traced here: 179 us
  Pallas kernels  61.2 us (34%)
  blocking collectives  35.8 us (20%)
  local copies, waits for them, and re-layouts  32.8 us (18%)
  waiting for transfers between devices  26.9 us (15%)
  starting transfers between devices  21.1 us (12%)
    pallas_call x1, Pallas kernels, body(): pl.pallas_call(functools.partial(local_part, cap), out_shape=(jax.ShapeDt...  38.5 us
    unnamed x48, local copies, waits for them, and re-layouts  32.8 us
    all_to_all x2, waiting for transfers between devices, send(): return lax.all_to_all(x, 'dom', split_axis=0, concat_axis=0, tiled=True)  26.9 us
    all_to_all x1, blocking collectives, send(): return lax.all_to_all(x, 'dom', split_axis=0, concat_axis=0, tiled=True)  22.4 us
    all_to_all x2, starting transfers between devices, send(): return lax.all_to_all(x, 'dom', split_axis=0, concat_axis=0, tiled=True)  21.1 us
    pallas_call x2, Pallas kernels, body(): pl.pallas_call(functools.partial(remote_part, classes, h, cap), out_shape...  16.9 us
    all_to_all x1, blocking collectives, body(): lax.all_to_all(mine, 'dir', split_axis=0, concat_axis=0, tiled=True)  13.4 us
  transfers between devices with their start and end apart: 2, of which 2 were waited for; matrix products, arithmetic and copies ran while one was open for 0% of the time, Pallas kernels for 28%

profile of v2, /device:TPU:1, one launch (start us, length us, event | category | flops | bytes accessed | tf_op | source)
XLA Modules:
  0.0 178.6 jit_solution(14324408646628402622)
XLA Ops:
  0.6 0.0 copy-start.7
  0.6 1.2 copy-done.7
  1.9 0.0 copy-start.11
  1.9 0.9 copy-done.11
  2.8 0.0 copy-start.21
  2.8 0.7 copy-done.21
  3.4 1.9 %pack_rows.3 = bf16[32,6,16,512]{3,2,1,0:T(8,128)(2,1)S(1)} custom-call(s32[8,32]{1,0:T(8,128)S(1)} %bitcast.7, f32[64,512]{1,0:T(8,128)S(1)} %copy-done.11, bf16[64,16,512]{2,1,0:T(8,128)(2,1)S(1)} %copy-done.7), custom_call_target="tpu_custom_call" | custom-call | flops 524288 | bytes 4194304 | tf_op jit(solution)/shard_map/pack_rows/pallas_call | solution.py:271
  5.4 0.0 copy-start.6
  5.4 1.7 copy-done.6
  7.0 0.0 copy-start.12
  7.0 0.0 copy-start.22
  7.0 0.0 copy-start.23
  7.0 12.2 %all-to-all-start.1 = ((bf16[32,6,16,512]{3,2,1,0:T(8,128)(2,1)}), bf16[32,6,16,512]{3,2,1,0:T(8,128)(2,1)S(1)}, u32[]{:S(2)}, u32[]{:S(2)}) async-start(bf16[32,6,16,512]{3,2,1,0:T(8,128)(2,1)} %copy-done.6), calls=%async_computation.1 | async-start | bytes 6291456 | tf_op jit(solution)/shard_map/all_to_all | solution.py:289
  19.2 0.0 copy-done.12
  19.2 0.0 copy-done.22
  19.2 0.0 copy-start.8
  19.2 1.2 copy-done.8
  20.4 1.3 pack_rows.2
  21.8 0.0 copy-start.10
  21.8 1.0 copy-done.10
  22.8 0.0 copy-done.23
  22.8 0.0 copy-start
  22.8 2.8 %copy-done = bf16[12,512,512]{2,1,0:T(8,128)(2,1)S(1)} copy-done((bf16[12,512,512]{2,1,0:T(8,128)(2,1)S(1)}, bf16[12,512,512]{2,1,0:T(8,128)(2,1)}, u32[]{:S(2)}) %copy-start) | copy-done | bytes 6291480
  25.5 0.0 copy-start.9
  25.5 1.2 copy-done.9
  26.8 0.0 copy-start.17
  26.8 1.2 copy-done.17
  28.0 38.5 %local_part.1 = (f32[1024,512]{1,0:T(8,128)S(1)}, bf16[257,16,512]{2,1,0:T(8,128)(2,1)S(1)}, f32[64,512]{1,0:T(8,128)S(1)}, s32[1728]{0:T(1024)S(1)}, s32[24]{0:T(128)S(1)}) custom-call(s32[12,64]{1,0:T(8,128)S(1)} %bitcast.10, bf16[64,16,512]{2,1,0:T(8,128)(2,1)S(1)} %copy-done.9, bf16[64,16,512]{2,1,0:T(8,128)(2,1)S(1)} %copy-done.17, ...), custom_call_target="tpu_custom_call" | custom-call | flops 12884901888 | bytes 16777216 | tf_op jit(solution)/shard_map/local_part/pallas_call | solution.py:292
  66.5 0.0 copy-start.3
  66.5 2.0 %copy-done.3 = bf16[257,16,512]{2,1,0:T(8,128)(2,1)} copy-done((bf16[257,16,512]{2,1,0:T(8,128)(2,1)}, bf16[257,16,512]{2,1,0:T(8,128)(2,1)S(1)}, u32[]{:S(2)}) %copy-start.3) | copy-done | bytes 4210712
  68.5 0.0 copy-start.13
  68.5 1.4 copy-done.13
  69.9 20.8 %all-to-all-done.1 = bf16[32,6,16,512]{3,2,1,0:T(8,128)(2,1)S(1)} async-done(((bf16[32,6,16,512]{3,2,1,0:T(8,128)(2,1)}), bf16[32,6,16,512]{3,2,1,0:T(8,128)(2,1)S(1)}, u32[]{:S(2)}, u32[]{:S(2)}) %all-to-all-start.1) | async-done | bytes 3145760 | tf_op jit(solution)/shard_map/all_to_all | solution.py:289
  90.7 8.9 %all-to-all-start = ((bf16[32,2,16,512]{3,2,1,0:T(8,128)(2,1)}), bf16[32,2,16,512]{3,2,1,0:T(8,128)(2,1)}, u32[]{:S(2)}, u32[]{:S(2)}) async-start(bf16[32,2,16,512]{3,2,1,0:T(8,128)(2,1)} %copy-done.10), calls=%async_computation | async-start | bytes 2097152 | tf_op jit(solution)/shard_map/all_to_all | solution.py:289
  99.7 0.0 copy-start.1
  99.7 2.8 %copy-done.1 = bf16[12,512,512]{2,1,0:T(8,128)(2,1)S(1)} copy-done((bf16[12,512,512]{2,1,0:T(8,128)(2,1)S(1)}, bf16[12,512,512]{2,1,0:T(8,128)(2,1)}, u32[]{:S(2)}) %copy-start.1) | copy-done | bytes 6291480
  102.4 0.0 copy-start.4
  102.4 2.2 %copy-done.4 = bf16[257,16,512]{2,1,0:T(8,128)(2,1)S(1)} copy-done((bf16[257,16,512]{2,1,0:T(8,128)(2,1)S(1)}, bf16[257,16,512]{2,1,0:T(8,128)(2,1)}, u32[]{:S(2)}) %copy-start.4) | copy-done | bytes 4210712
  104.6 0.0 copy-start.14
  104.6 1.6 copy-done.14
  106.2 9.8 %remote_part.2 = (f32[1024,512]{1,0:T(8,128)S(1)}, f32[32,8,512]{2,1,0:T(8,128)S(1)}) custom-call(s32[1728]{0:T(1024)S(1)} %get-tuple-element.14.order_ref, s32[24]{0:T(128)S(1)} %get-tuple-element.15.count_ref, bf16[192,16,512]{2,1,0:T(8,128)(2,1)S(1)} %bitcast.6, bf16[257,16,512]{2,1,0:T(8,128)(2,1)S(1)} %copy-done.4, f32[1024,512]{1,0:T(8,128)S(1)} %copy-done.14, ...), custom_call_target="tpu_custom_call" | custom-call | flops 1610612736 | bytes 14680064 | tf_op jit(solution)/shard_map/remote_part/pallas_call | solution.py:334
  116.0 0.0 copy-start.15
  116.0 1.4 copy-done.15
  117.4 0.0 copy-start.19
  117.4 0.8 copy-done.19
  118.2 6.1 %all-to-all-done = bf16[32,2,16,512]{3,2,1,0:T(8,128)(2,1)} async-done(((bf16[32,2,16,512]{3,2,1,0:T(8,128)(2,1)}), bf16[32,2,16,512]{3,2,1,0:T(8,128)(2,1)}, u32[]{:S(2)}, u32[]{:S(2)}) %all-to-all-start) | async-done | bytes 1048608 | tf_op jit(solution)/shard_map/all_to_all | solution.py:289
  124.3 0.0 copy-start.2
  124.3 2.8 %copy-done.2 = bf16[12,512,512]{2,1,0:T(8,128)(2,1)S(1)} copy-done((bf16[12,512,512]{2,1,0:T(8,128)(2,1)S(1)}, bf16[12,512,512]{2,1,0:T(8,128)(2,1)}, u32[]{:S(2)}) %copy-start.2) | copy-done | bytes 6291480
  127.1 0.0 copy-start.5
  127.1 2.2 %copy-done.5 = bf16[257,16,512]{2,1,0:T(8,128)(2,1)S(1)} copy-done((bf16[257,16,512]{2,1,0:T(8,128)(2,1)S(1)}, bf16[257,16,512]{2,1,0:T(8,128)(2,1)}, u32[]{:S(2)}) %copy-start.5) | copy-done | bytes 4210712
  129.3 0.0 copy-start.16
  129.3 1.6 copy-done.16
  130.9 0.0 copy-start.18
  130.9 1.2 copy-done.18
  132.1 0.0 copy-start.20
  132.1 1.0 copy-done.20
  133.1 7.1 %remote_part.3 = (bf16[64,16,512]{2,1,0:T(8,128)(2,1)}, f32[64,512]{1,0:T(8,128)S(1)}, f32[32,8,512]{2,1,0:T(8,128)S(1)}) custom-call(s32[1728]{0:T(1024)S(1)} %get-tuple-element.14.order_ref, s32[24]{0:T(128)S(1)} %get-tuple-element.15.count_ref, bf16[64,16,512]{2,1,0:T(8,128)(2,1)} %bitcast.3.arrived_ref, bf16[257,16,512]{2,1,0:T(8,128)(2,1)S(1)} %copy-done.5, ...), custom_call_target="tpu_custom_call" | custom-call | flops 536870912 | bytes 14680064 | tf_op jit(solution)/shard_map/remote_part/pallas_call | solution.py:334
  140.3 22.4 %all_to_all.20.term_ref = f32[32,8,512]{2,1,0:T(8,128)S(1)} all-to-all(f32[32,8,512]{2,1,0:T(8,128)S(1)} %get-tuple-element.25), channel_id=1, replica_groups=mesh['dom'=32,'dir'=8] {'dom'}, dimensions={0} | all-to-all | bytes 1048576 | tf_op jit(solution)/shard_map/all_to_all | solution.py:289
  162.7 1.9 %combine.1 = f32[8,32,128]{2,1,0:T(8,128)S(1)} custom-call(s32[8,32]{1,0:T(8,128)S(1)} %bitcast.9, f32[64,512]{1,0:T(8,128)S(1)} %copy-done.12, f32[64,512]{1,0:T(8,128)S(1)} %get-tuple-element.24.part_ref, f32[32,8,512]{2,1,0:T(8,128)S(1)} %all_to_all.20.term_ref), custom_call_target="tpu_custom_call" | custom-call | flops 524288 | bytes 1048576 | tf_op jit(solution)/shard_map/combine/pallas_call | solution.py:353
  164.6 13.4 %all_to_all.21.in_ref = f32[8,32,128]{2,1,0:T(8,128)S(1)} all-to-all(f32[8,32,128]{2,1,0:T(8,128)S(1)} %combine.1), channel_id=1, replica_groups=mesh['dom'=32,'dir'=8] {'dir'}, dimensions={0} | all-to-all | bytes 262144 | tf_op jit(solution)/shard_map/all_to_all | solution.py:363
  177.9 0.7 add_shares.1
Async XLA Ops:
  0.6 1.2 copy-start.7
  1.9 0.9 copy-start.11
  2.8 0.7 copy-start.21
  5.4 1.7 copy-start.6
  7.0 12.2 %copy-start.12 = (f32[64,512]{1,0:T(8,128)S(1)}, f32[64,512]{1,0:T(8,128)}, u32[]{:S(2)}) copy-start(f32[64,512]{1,0:T(8,128)} %mie_ref.3) | copy-start | bytes 393220
  7.0 12.2 %copy-start.22 = (s32[1,32,8]{1,2,0:T(8,128)S(1)}, s32[1,32,8]{1,2,0:T(8,128)}, u32[]{:S(2)}) copy-start(s32[1,32,8]{1,2,0:T(8,128)} %param.10) | copy-start | bytes 3076
  7.0 15.7 %copy-start.23 = (s32[64,12]{0,1:T(8,128)S(1)}, s32[64,12]{0,1:T(8,128)}, u32[]{:S(2)}) copy-start(s32[64,12]{0,1:T(8,128)} %param.11) | copy-start | bytes 9220
  7.0 83.7 %all-to-all-start.1 = ((bf16[32,6,16,512]{3,2,1,0:T(8,128)(2,1)}), bf16[32,6,16,512]{3,2,1,0:T(8,128)(2,1)S(1)}, u32[]{:S(2)}, u32[]{:S(2)}) async-start(bf16[32,6,16,512]{3,2,1,0:T(8,128)(2,1)} %copy-done.6), calls=%async_computation.1 | async-start | bytes 6291456 | tf_op jit(solution)/shard_map/all_to_all | solution.py:289
  19.2 1.2 copy-start.8
  21.8 1.0 copy-start.10
  22.8 2.8 %copy-start = (bf16[12,512,512]{2,1,0:T(8,128)(2,1)S(1)}, bf16[12,512,512]{2,1,0:T(8,128)(2,1)}, u32[]{:S(2)}) copy-start(bf16[12,512,512]{2,1,0:T(8,128)(2,1)} %trans_ref.5) | copy-start | bytes 18874372
  25.5 1.2 copy-start.9
  26.8 1.2 copy-start.17
  66.5 2.0 %copy-start.3 = (bf16[257,16,512]{2,1,0:T(8,128)(2,1)}, bf16[257,16,512]{2,1,0:T(8,128)(2,1)S(1)}, u32[]{:S(2)}) copy-start(bf16[257,16,512]{2,1,0:T(8,128)(2,1)S(1)} %get-tuple-element.18.back_ref) | copy-start | bytes 12632068
  68.5 1.4 copy-start.13
  90.7 33.6 %all-to-all-start = ((bf16[32,2,16,512]{3,2,1,0:T(8,128)(2,1)}), bf16[32,2,16,512]{3,2,1,0:T(8,128)(2,1)}, u32[]{:S(2)}, u32[]{:S(2)}) async-start(bf16[32,2,16,512]{3,2,1,0:T(8,128)(2,1)} %copy-done.10), calls=%async_computation | async-start | bytes 2097152 | tf_op jit(solution)/shard_map/all_to_all | solution.py:289
  99.7 2.8 %copy-start.1 = (bf16[12,512,512]{2,1,0:T(8,128)(2,1)S(1)}, bf16[12,512,512]{2,1,0:T(8,128)(2,1)}, u32[]{:S(2)}) copy-start(bf16[12,512,512]{2,1,0:T(8,128)(2,1)} %trans_ref.5) | copy-start | bytes 18874372
  102.4 2.2 %copy-start.4 = (bf16[257,16,512]{2,1,0:T(8,128)(2,1)S(1)}, bf16[257,16,512]{2,1,0:T(8,128)(2,1)}, u32[]{:S(2)}) copy-start(bf16[257,16,512]{2,1,0:T(8,128)(2,1)} %copy-done.3) | copy-start | bytes 12632068
  104.6 1.6 copy-start.14
  116.0 1.4 copy-start.15
  117.4 0.8 copy-start.19
  124.3 2.8 %copy-start.2 = (bf16[12,512,512]{2,1,0:T(8,128)(2,1)S(1)}, bf16[12,512,512]{2,1,0:T(8,128)(2,1)}, u32[]{:S(2)}) copy-start(bf16[12,512,512]{2,1,0:T(8,128)(2,1)} %trans_ref.5) | copy-start | bytes 18874372
  127.1 2.2 %copy-start.5 = (bf16[257,16,512]{2,1,0:T(8,128)(2,1)S(1)}, bf16[257,16,512]{2,1,0:T(8,128)(2,1)}, u32[]{:S(2)}) copy-start(bf16[257,16,512]{2,1,0:T(8,128)(2,1)} %copy-done.3) | copy-start | bytes 12632068
  129.3 1.6 copy-start.16
  130.9 1.2 copy-start.18
  132.1 1.0 copy-start.20

commit v3 on v2

v3 whole, which is shorter than its diff:
```python
import functools

import jax
import jax.numpy as jnp
from jax import lax
from jax.experimental import pallas as pl
from jax.experimental.pallas import tpu as pltpu
from jax.sharding import PartitionSpec as P

TILE = 24
WINDOW = 3
LANES = 128
PARTS = 8
F32 = jnp.float32
BF16 = jnp.bfloat16
MIB = 1 << 20


def vmem():
    return pl.BlockSpec(memory_space=pltpu.VMEM)


def smem():
    return pl.BlockSpec(memory_space=pltpu.SMEM)


def hbm():
    return pl.BlockSpec(memory_space=pl.ANY)


def pack_rows(
    rows_hbm, mie_hbm, inc_hbm, out_hbm, rows_ref, mie_ref, inc_ref, start_ref, out_ref, in_sem, out_sem
):
    peers, cap = out_ref.shape[:2]
    part_peers = peers // PARTS
    gets = [
        pltpu.make_async_copy(inc_hbm, inc_ref, in_sem.at[0]),
        pltpu.make_async_copy(mie_hbm, mie_ref, in_sem.at[1]),
        pltpu.make_async_copy(rows_hbm, rows_ref, in_sem.at[2]),
    ]
    for get in gets:
        get.start()
    for get in gets:
        get.wait()

    def scale(p, carry):
        start_ref[p] = (mie_ref[pl.ds(p, 1), :] * inc_ref[p].astype(F32)).astype(BF16)
        return carry

    lax.fori_loop(0, inc_ref.shape[0], scale, 0, unroll=8)

    def put(part):
        here = pl.ds(part * part_peers, part_peers)
        return pltpu.make_async_copy(out_ref.at[here], out_hbm.at[here], out_sem.at[part])

    for part in range(PARTS):
        for i in range(part_peers):
            peer = part * part_peers + i
            for c in range(cap):
                out_ref[peer, c] = start_ref[rows_ref[c, peer]]
        put(part).start()
    for part in range(PARTS):
        put(part).wait()


def local_part(
    slot_ref,
    rows_ref,
    inc_hbm,
    cot_hbm,
    mie_hbm,
    trans_hbm,
    field_ref,
    back_ref,
    grad_ref,
    owner_ref,
    order_ref,
    count_ref,
    inc_ref,
    cot_ref,
    mie_ref,
    trans_ref,
    start_ref,
    adj_ref,
    lhs_ref,
    prod_ref,
    adjoint_ref,
    in_sem,
    trans_sem,
):
    count_p, count_n, width = inc_ref.shape
    classes = slot_ref.shape[0]
    stride = count_p + TILE
    dummy = back_ref.shape[0] - 1
    gets = [
        pltpu.make_async_copy(mie_hbm, mie_ref, in_sem.at[0]),
        pltpu.make_async_copy(inc_hbm, inc_ref, in_sem.at[1]),
        pltpu.make_async_copy(cot_hbm, cot_ref, in_sem.at[2]),
    ]

    def get_trans(k):
        return pltpu.make_async_copy(trans_hbm.at[k], trans_ref.at[k], trans_sem.at[k])

    for get in gets:
        get.start()
    for k in range(classes):
        get_trans(k).start()
    for get in gets:
        get.wait()

    def prepare(p, carry):
        scale = mie_ref[pl.ds(p, 1), :]
        inc = inc_ref[p].astype(F32)
        start_ref[p] = (scale * inc).astype(BF16)
        at = pl.multiple_of(p * count_n, count_n)
        adj_ref[pl.ds(at, count_n), :] = (scale * cot_ref[p].astype(F32)).astype(BF16)
        field_ref[pl.ds(at, count_n), :] = inc
        adjoint_ref[p] = jnp.zeros((count_n, width), F32)
        return carry

    lax.fori_loop(0, count_p, prepare, 0, unroll=4)
    start_ref[count_p] = jnp.zeros((count_n, width), BF16)
    adjoint_ref[count_p] = jnp.zeros((count_n, width), F32)

    def one_class(k, carry):
        base = k * stride

        def pick(p, tally):
            slot = slot_ref[k, p]
            is_local = (slot >= 0) & (slot < count_p)
            source = jnp.where(is_local, slot, count_p)
            at = pl.multiple_of(p * count_n, count_n)
            lhs_ref[pl.ds(at, count_n), :] = start_ref[source]
            remote = slot - count_p
            order_ref[base + tally] = remote * 128 + p
            return tally + (remote >= 0).astype(jnp.int32)

        tally = lax.fori_loop(0, count_p, pick, jnp.int32(0), unroll=4)
        count_ref[k] = tally
        for extra in range(TILE):
            order_ref[base + tally + extra] = count_p
        get_trans(k).wait()
        field_ref[...] += jnp.dot(lhs_ref[...], trans_ref[k], preferred_element_type=F32)
        prod_ref[...] = lax.dot_general(
            adj_ref[...],
            trans_ref[k],
            (((1,), (1,)), ((), ())),
            preferred_element_type=F32,
        )

        def spread(p, c):
            slot = slot_ref[k, p]
            is_local = (slot >= 0) & (slot < count_p)
            at = pl.multiple_of(p * count_n, count_n)
            prod = prod_ref[pl.ds(at, count_n), :]
            back_ref[jnp.where(slot >= count_p, slot - count_p, dummy)] = prod.astype(BF16)
            adjoint_ref[jnp.where(is_local, slot, count_p)] += prod
            return c

        lax.fori_loop(0, count_p, spread, 0, unroll=4)
        return carry

    lax.fori_loop(0, classes, one_class, 0)

    def own(q, carry):
        lane = lax.broadcasted_iota(jnp.int32, (1, LANES), 1)
        for c in range(rows_ref.shape[0]):
            owner_ref[pl.ds(q * rows_ref.shape[0] + c, 1), :] = (lane == rows_ref[c, q]).astype(F32)
        return carry

    lax.fori_loop(0, rows_ref.shape[1], own, 0)

    def finish(p, carry):
        at = pl.multiple_of(p * count_n, count_n)
        both = inc_ref[p].astype(F32) * adjoint_ref[p]
        both += cot_ref[p].astype(F32) * field_ref[pl.ds(at, count_n), :]
        grad_ref[pl.ds(p, 1), :] = jnp.sum(both, axis=0, keepdims=True)
        return carry

    lax.fori_loop(0, count_p, finish, 0, unroll=4)


def remote_terms(arrived_hbm, back_hbm, term_ref, arrived_ref, back_ref, sem):
    peers, cap = term_ref.shape[:2]
    part_peers = peers // PARTS

    def get(part):
        here = pl.ds(part * part_peers * cap, part_peers * cap)
        return (
            pltpu.make_async_copy(arrived_hbm.at[here], arrived_ref.at[here], sem.at[0, part]),
            pltpu.make_async_copy(back_hbm.at[here], back_ref.at[here], sem.at[1, part]),
        )

    for part in range(PARTS):
        for copy in get(part):
            copy.start()
    for part in range(PARTS):
        for copy in get(part):
            copy.wait()

        def one(i, carry, part=part):
            peer = part * part_peers + i
            here = pl.ds(peer * cap, cap)
            both = arrived_ref[here].astype(F32) * back_ref[here].astype(F32)
            term_ref[peer] = jnp.sum(both, axis=1).astype(BF16)
            return carry

        lax.fori_loop(0, part_peers, one, 0)


def remote_field(
    order_ref,
    count_ref,
    arrived_hbm,
    trans_hbm,
    cot_hbm,
    part_hbm,
    acc_ref,
    grad_hbm,
    arrived_ref,
    trans_ref,
    cot_ref,
    part_ref,
    grad_ref,
    lhs_even,
    lhs_odd,
    moved_even,
    moved_odd,
    in_sem,
    trans_sem,
    out_sem,
):
    classes = trans_ref.shape[0]
    count_p, count_n, width = cot_ref.shape
    stride = count_p + TILE
    get_arrived = pltpu.make_async_copy(arrived_hbm, arrived_ref, in_sem.at[0])
    late = [
        pltpu.make_async_copy(cot_hbm, cot_ref, in_sem.at[1]),
        pltpu.make_async_copy(part_hbm, part_ref, in_sem.at[2]),
    ]

    def get_trans(k):
        return pltpu.make_async_copy(trans_hbm.at[k], trans_ref.at[k], trans_sem.at[k])

    get_arrived.start()
    for k in range(WINDOW):
        get_trans(k).start()

    def clear(p, carry):
        at = pl.multiple_of(p * count_n, count_n)
        acc_ref[pl.ds(at, count_n), :] = jnp.zeros((count_n, width), F32)
        return carry

    lax.fori_loop(0, count_p + 1, clear, 0, unroll=5)
    moved_odd[...] = jnp.zeros_like(moved_odd)
    get_arrived.wait()

    def gather(k, lhs, t=0):
        base = k * stride + t * TILE
        for i in range(TILE):
            source = lax.shift_right_logical(order_ref[base + i], 7)
            lhs[pl.ds(i * count_n, count_n), :] = arrived_ref[source]

    def scatter(k, moved, t=0):
        base = k * stride + t * TILE
        for i in range(TILE):
            p = order_ref[base + i] & 127
            at = pl.multiple_of(p * count_n, count_n)
            acc_ref[pl.ds(at, count_n), :] += moved[pl.ds(i * count_n, count_n), :]

    def fetch(k):
        get_trans(k).wait()

        @pl.when(k + WINDOW < classes)
        def _():
            get_trans(k + WINDOW).start()

        @pl.when(k + WINDOW == classes)
        def _():
            for get in late:
                get.start()

    gather(0, lhs_even)

    def two_classes(i, carry):
        k = 2 * i
        fetch(k)
        moved_even[...] = jnp.dot(lhs_even[...], trans_ref[k], preferred_element_type=F32)
        gather(k + 1, lhs_odd)
        scatter(jnp.maximum(k - 1, 0), moved_odd)
        fetch(k + 1)
        moved_odd[...] = jnp.dot(lhs_odd[...], trans_ref[k + 1], preferred_element_type=F32)
        gather(jnp.minimum(k + 2, classes - 1), lhs_even)
        scatter(k, moved_even)
        return carry

    lax.fori_loop(0, classes // 2, two_classes, 0)
    scatter(classes - 1, moved_odd)

    def more(k, carry):
        def one_tile(t, c):
            gather(k, lhs_even, t)
            moved_even[...] = jnp.dot(lhs_even[...], trans_ref[k], preferred_element_type=F32)
            scatter(k, moved_even, t)
            return c

        lax.fori_loop(1, lax.div(count_ref[k] + (TILE - 1), TILE), one_tile, 0)
        return carry

    lax.fori_loop(0, classes, more, 0)
    for get in late:
        get.wait()

    def finish(p, carry):
        at = pl.multiple_of(p * count_n, count_n)
        grad_ref[pl.ds(p, 1), :] = part_ref[pl.ds(p, 1), :] + jnp.sum(
            cot_ref[p].astype(F32) * acc_ref[pl.ds(at, count_n), :], axis=0, keepdims=True
        )
        return carry

    lax.fori_loop(0, count_p, finish, 0, unroll=4)
    put = pltpu.make_async_copy(grad_ref, grad_hbm, out_sem)
    put.start()
    put.wait()


def amplitudes(acc_ref, field_hbm, mie_hbm, amp_hbm, field_ref, mie_ref, amp_ref, in_sem, out_sem):
    count_p, count_n, width = amp_ref.shape
    step = count_p // PARTS

    def get(part):
        here = pl.ds(part * step * count_n, step * count_n)
        return pltpu.make_async_copy(field_hbm.at[here], field_ref.at[here], in_sem.at[part])

    def put(part):
        here = pl.ds(part * step, step)
        return pltpu.make_async_copy(amp_ref.at[here], amp_hbm.at[here], out_sem.at[part])

    get_mie = pltpu.make_async_copy(mie_hbm, mie_ref, in_sem.at[PARTS])
    get_mie.start()
    for part in range(PARTS):
        get(part).start()
    get_mie.wait()
    for part in range(PARTS):
        get(part).wait()

        def one(i, carry, part=part):
            p = part * step + i
            here = pl.ds(pl.multiple_of(p * count_n, count_n), count_n)
            field = field_ref[here, :] + acc_ref[here, :]
            amp_ref[p] = (mie_ref[pl.ds(p, 1), :] * field).astype(BF16)
            return carry

        lax.fori_loop(0, step, one, 0, unroll=4)
        put(part).start()
    for part in range(PARTS):
        put(part).wait()


def combine(scale, owner_hbm, mie_hbm, part_hbm, term_ref, out_ref, owner_ref, mie_ref, part_ref, sem):
    gets = [
        pltpu.make_async_copy(owner_hbm, owner_ref, sem.at[0]),
        pltpu.make_async_copy(mie_hbm, mie_ref, sem.at[1]),
        pltpu.make_async_copy(part_hbm, part_ref, sem.at[2]),
    ]
    for get in gets:
        get.start()
    for get in gets:
        get.wait()
    count_p, width = mie_ref.shape
    mine = lax.dot_general(
        owner_ref[...].astype(BF16),
        term_ref[...].reshape(owner_ref.shape[0], width),
        (((0,), (0,)), ((), ())),
        preferred_element_type=F32,
    )
    whole = (part_ref[...] + mine[:count_p] / mie_ref[...]) * scale
    dirs, half, pair = out_ref.shape
    share = pair // 2
    for r in range(dirs):
        block = whole[:, r * share : (r + 1) * share]
        out_ref[r] = jnp.concatenate([block[:half], block[half:]], axis=1)


def add_shares(in_ref, out_ref):
    summed = jnp.sum(in_ref[...], axis=0)
    share = summed.shape[1] // 2
    out_ref[...] = jnp.concatenate([summed[:, :share], summed[:, share:]], axis=0)


def params(mib=60):
    return pltpu.CompilerParams(vmem_limit_bytes=mib * MIB)


def cost(flops, mib):
    return pl.CostEstimate(flops=int(flops), bytes_accessed=mib * MIB, transcendentals=0)


def stay(x):
    return pltpu.with_memory_space_constraint(x, pltpu.VMEM)


def body(incident, cotangent, mie, trans, send_rows, partner_slot):
    count_p, count_n, width = incident.shape
    classes = trans.shape[0]
    peers = lax.axis_size("dom")
    dirs = lax.axis_size("dir")
    cap = send_rows.shape[2]
    remote_rows = peers * cap
    total = count_p * count_n
    row_ops = count_p * count_n * width

    rows = jnp.transpose(send_rows[0])
    slots = jnp.transpose(partner_slot)

    def send(x):
        return lax.all_to_all(x, "dom", split_axis=0, concat_axis=0, tiled=True)

    packed = pl.pallas_call(
        pack_rows,
        out_shape=jax.ShapeDtypeStruct((peers, cap, count_n, width), BF16),
        in_specs=[hbm()] * 3,
        out_specs=hbm(),
        scratch_shapes=[
            pltpu.SMEM((cap, peers), jnp.int32),
            pltpu.VMEM((count_p, width), F32),
            pltpu.VMEM((count_p, count_n, width), BF16),
            pltpu.VMEM((count_p, count_n, width), BF16),
            pltpu.VMEM((peers, cap, count_n, width), BF16),
            pltpu.SemaphoreType.DMA((3,)),
            pltpu.SemaphoreType.DMA((PARTS,)),
        ],
        compiler_params=params(),
        cost_estimate=cost(row_ops, 4),
        name="pack_rows",
    )(rows, mie, incident)
    arrived = send(packed).reshape(remote_rows, count_n, width)

    field, back, part, owner, order, count = pl.pallas_call(
        local_part,
        out_shape=(
            jax.ShapeDtypeStruct((total, width), F32),
            jax.ShapeDtypeStruct((remote_rows + 1, count_n, width), BF16),
            jax.ShapeDtypeStruct((count_p, width), F32),
            jax.ShapeDtypeStruct((remote_rows, LANES), F32),
            jax.ShapeDtypeStruct((classes * (count_p + TILE),), jnp.int32),
            jax.ShapeDtypeStruct((classes,), jnp.int32),
        ),
        in_specs=[smem(), smem()] + [hbm()] * 4,
        out_specs=(vmem(),) * 4 + (smem(),) * 2,
        scratch_shapes=[
            pltpu.VMEM((count_p, count_n, width), BF16),
            pltpu.VMEM((count_p, count_n, width), BF16),
            pltpu.VMEM((count_p, width), F32),
            pltpu.VMEM((classes, width, width), BF16),
            pltpu.VMEM((count_p + 1, count_n, width), BF16),
            pltpu.VMEM((total, width), BF16),
            pltpu.VMEM((total, width), BF16),
            pltpu.VMEM((total, width), F32),
            pltpu.VMEM((count_p + 1, count_n, width), F32),
            pltpu.SemaphoreType.DMA((3,)),
            pltpu.SemaphoreType.DMA((classes,)),
        ],
        compiler_params=params(),
        cost_estimate=cost(4 * classes * row_ops * width, 16),
        name="local_part",
    )(slots, rows, incident, cotangent, mie, trans)

    term = pl.pallas_call(
        remote_terms,
        out_shape=jax.ShapeDtypeStruct((peers, cap, width), BF16),
        in_specs=[hbm(), hbm()],
        out_specs=vmem(),
        scratch_shapes=[
            pltpu.VMEM((remote_rows, count_n, width), BF16),
            pltpu.VMEM((remote_rows, count_n, width), BF16),
            pltpu.SemaphoreType.DMA((2, PARTS)),
        ],
        compiler_params=params(),
        cost_estimate=cost(4 * row_ops, 8),
        name="remote_terms",
    )(arrived, back)
    term = send(term)

    acc, part = pl.pallas_call(
        remote_field,
        out_shape=(
            pltpu.VMEM((total + count_n, width), F32),
            jax.ShapeDtypeStruct((count_p, width), F32),
        ),
        in_specs=[smem(), smem()] + [hbm()] * 4,
        out_specs=(vmem(), hbm()),
        scratch_shapes=[
            pltpu.VMEM((remote_rows, count_n, width), BF16),
            pltpu.VMEM((classes, width, width), BF16),
            pltpu.VMEM((count_p, count_n, width), BF16),
            pltpu.VMEM((count_p, width), F32),
            pltpu.VMEM((count_p, width), F32),
            pltpu.VMEM((TILE * count_n, width), BF16),
            pltpu.VMEM((TILE * count_n, width), BF16),
            pltpu.VMEM((TILE * count_n, width), F32),
            pltpu.VMEM((TILE * count_n, width), F32),
            pltpu.SemaphoreType.DMA((3,)),
            pltpu.SemaphoreType.DMA((classes,)),
            pltpu.SemaphoreType.DMA,
        ],
        compiler_params=params(56),
        cost_estimate=cost(2 * remote_rows * count_n * width * width, 14),
        name="remote_field",
    )(order, count, arrived, trans, cotangent, part)
    acc = stay(acc)

    mine = pl.pallas_call(
        functools.partial(combine, 1.0 / (count_n * dirs)),
        out_shape=jax.ShapeDtypeStruct((dirs, count_p // 2, 2 * width // dirs), F32),
        in_specs=[hbm()] * 3 + [vmem()],
        out_specs=vmem(),
        scratch_shapes=[
            pltpu.VMEM((remote_rows, LANES), F32),
            pltpu.VMEM((count_p, width), F32),
            pltpu.VMEM((count_p, width), F32),
            pltpu.SemaphoreType.DMA((3,)),
        ],
        compiler_params=params(24),
        cost_estimate=cost(row_ops, 1),
        name="combine",
    )(owner, mie, part, term)
    mine, field = lax.optimization_barrier((mine, field))
    amplitude = pl.pallas_call(
        amplitudes,
        out_shape=jax.ShapeDtypeStruct((count_p, count_n, width), BF16),
        in_specs=[vmem(), hbm(), hbm()],
        out_specs=hbm(),
        scratch_shapes=[
            pltpu.VMEM((total, width), F32),
            pltpu.VMEM((count_p, width), F32),
            pltpu.VMEM((count_p, count_n, width), BF16),
            pltpu.SemaphoreType.DMA((PARTS + 1,)),
            pltpu.SemaphoreType.DMA((PARTS,)),
        ],
        compiler_params=params(56),
        cost_estimate=cost(row_ops, 5),
        name="amplitudes",
    )(acc, field, mie)
    shares = lax.all_to_all(mine, "dir", split_axis=0, concat_axis=0, tiled=True)
    gradient = pl.pallas_call(
        add_shares,
        out_shape=jax.ShapeDtypeStruct((count_p, width // dirs), F32),
        in_specs=[vmem()],
        out_specs=vmem(),
        compiler_params=params(8),
        cost_estimate=cost(row_ops, 1),
        name="add_shares",
    )(shares)
    return amplitude, gradient


def solution(mesh):
    placed = (
        P("dom", "dir", None),
        P("dom", "dir", None),
        P("dom", None),
        P(),
        P("dom", None, None),
        P("dom", None),
    )
    return jax.shard_map(
        body,
        mesh=mesh,
        in_specs=placed,
        out_specs=(P("dom", "dir", None), P("dom", "dir")),
        check_vma=False,
    )
```

time: 180 us -> 149 us (0.83)
  blocking collectives: 35.8 us -> 0 us
  waiting for transfers between devices: 26.9 us -> 59.4 us
  local copies, waits for them, and re-layouts: 32.8 us -> 0.91 us
  starting transfers between devices: 21.1 us -> 27.3 us
    all_to_all x2 -> x0, blocking collectives: 35.8 us -> none  [the longest x1 22.4 us: send(): return lax.all_to_all(x, 'dom', split_axis=0, concat_axis=0, tiled=True)]
    unnamed x48 -> x6, local copies, waits for them, and re-layouts: 32.8 us -> 0.91 us
    all_to_all x2, waiting for transfers between devices: 26.9 us -> 56.5 us  [send(): return lax.all_to_all(x, 'dom', split_axis=0, concat_axis=0, tiled=True)]
    all_to_all x0 -> x1, starting transfers between devices: none -> 5.86 us  [body(): lax.all_to_all(mine, 'dir', split_axis=0, concat_axis=0, tiled=True)]
    all_to_all x0 -> x1, waiting for transfers between devices: none -> 2.85 us  [body(): lax.all_to_all(mine, 'dir', split_axis=0, concat_axis=0, tiled=True)]
  transfers between devices with their start and end apart: 2 -> 3, of which waited for: 2 -> 2; matrix products, arithmetic and copies ran while one was open for 0% -> 0% of each run, Pallas kernels for 28% -> 34%
where the time goes in v3:
time: 149 us
  Pallas kernels  60.5 us (41%)
  waiting for transfers between devices  59.4 us (40%)
  starting transfers between devices  27.3 us (18%)
    all_to_all x2, waiting for transfers between devices, send(): return lax.all_to_all(x, 'dom', split_axis=0, concat_axis=0, tiled=True)  56.5 us
    pallas_call x1, Pallas kernels, body(): pl.pallas_call(local_part, out_shape=(jax.ShapeDtypeStruct((total, width)...  36.2 us
    all_to_all x2, starting transfers between devices, send(): return lax.all_to_all(x, 'dom', split_axis=0, concat_axis=0, tiled=True)  21.4 us
    pallas_call x1, Pallas kernels, body(): pl.pallas_call(remote_field, out_shape=(pltpu.VMEM((total + count_n, widt...  11.7 us
    all_to_all x1, starting transfers between devices, body(): lax.all_to_all(mine, 'dir', split_axis=0, concat_axis=0, tiled=True)  5.86 us
    pallas_call x1, Pallas kernels, body(): pl.pallas_call(remote_terms, out_shape=jax.ShapeDtypeStruct((peers, cap,...  4.5 us
    pallas_call x1, Pallas kernels, body(): pl.pallas_call(pack_rows, out_shape=jax.ShapeDtypeStruct((peers, cap, cou...  3.54 us
  transfers between devices with their start and end apart: 3, of which 2 were waited for; matrix products, arithmetic and copies ran while one was open for 0% of the time, Pallas kernels for 34%

profile of v3, /device:TPU:1, one launch (start us, length us, event | category | flops | bytes accessed | tf_op | source)
XLA Modules:
  0.0 148.8 jit_solution(13553532748042685350)
XLA Ops:
  0.6 3.5 %pack_rows.1 = bf16[32,8,16,512]{3,2,1,0:T(8,128)(2,1)} custom-call(s32[8,32]{1,0:T(8,128)} %bitcast.5, f32[64,512]{1,0:T(8,128)} %mie_hbm.7, bf16[64,16,512]{2,1,0:T(8,128)(2,1)} %inc_hbm.3), custom_call_target="tpu_custom_call" | custom-call | flops 524288 | bytes 4194304 | tf_op jit(solution)/shard_map/pack_rows/pallas_call | solution.py:419
  4.2 12.2 %all-to-all-start = ((bf16[32,8,16,512]{3,2,1,0:T(8,128)(2,1)}), bf16[32,8,16,512]{3,2,1,0:T(8,128)(2,1)}, u32[]{:S(2)}, u32[]{:S(2)}) async-start(bf16[32,8,16,512]{3,2,1,0:T(8,128)(2,1)} %pack_rows.1), calls=%async_computation | async-start | bytes 8388608 | tf_op jit(solution)/shard_map/all_to_all | solution.py:417
  16.4 36.2 %local_part.1 = (f32[1024,512]{1,0:T(8,128)}, bf16[257,16,512]{2,1,0:T(8,128)(2,1)}, f32[64,512]{1,0:T(8,128)}, f32[256,128]{1,0:T(8,128)}, s32[1056]{0:T(1024)}, /*index=5*/s32[12]{0:T(128)}) custom-call(s32[12,64]{1,0:T(8,128)} %bitcast.7, s32[8,32]{1,0:T(8,128)} %bitcast.6, bf16[64,16,512]{2,1,0:T(8,128)(2,1)} %inc_hbm.3, bf16[64,16,512]{2,1,0:T(8,128)(2,1)} %cot_hbm.3, ...), custom_call_target="tpu_custom_call" | custom-call | flops 12884901888 | bytes 16777216 | tf_op jit(solution)/shard_map/local_part/pallas_call | solution.py:439
  52.6 56.5 %all-to-all-done = bf16[32,8,16,512]{3,2,1,0:T(8,128)(2,1)} async-done(((bf16[32,8,16,512]{3,2,1,0:T(8,128)(2,1)}), bf16[32,8,16,512]{3,2,1,0:T(8,128)(2,1)}, u32[]{:S(2)}, u32[]{:S(2)}) %all-to-all-start) | async-done | bytes 4194336 | tf_op jit(solution)/shard_map/all_to_all | solution.py:417
  109.1 4.5 %remote_terms.1 = bf16[32,8,512]{2,1,0:T(8,128)(2,1)} custom-call(bf16[256,16,512]{2,1,0:T(8,128)(2,1)} %bitcast.4.arrived_hbm, bf16[257,16,512]{2,1,0:T(8,128)(2,1)} %get-tuple-element.18.back_hbm), custom_call_target="tpu_custom_call" | custom-call | flops 2097152 | bytes 8388608 | tf_op jit(solution)/shard_map/remote_terms/pallas_call | solution.py:469
  113.6 9.2 %all-to-all-start.1 = ((bf16[32,8,512]{2,1,0:T(8,128)(2,1)}), bf16[32,8,512]{2,1,0:T(8,128)(2,1)S(1)}, u32[]{:S(2)}, u32[]{:S(2)}) async-start(bf16[32,8,512]{2,1,0:T(8,128)(2,1)} %remote_terms.1), calls=%async_computation.1 | async-start | bytes 524288 | tf_op jit(solution)/shard_map/all_to_all | solution.py:417
  122.9 0.0 copy-start
  122.9 0.0 copy-start.1
  122.9 11.7 %remote_field.1 = (f32[1040,512]{1,0:T(8,128)S(1)}, f32[64,512]{1,0:T(8,128)}) custom-call(s32[1056]{0:T(1024)} %get-tuple-element.12.order_ref, s32[12]{0:T(128)} %get-tuple-element.13.count_ref, bf16[256,16,512]{2,1,0:T(8,128)(2,1)} %bitcast.4.arrived_hbm, bf16[12,512,512]{2,1,0:T(8,128)(2,1)} %trans_hbm.3, bf16[64,16,512]{2,1,0:T(8,128)(2,1)} %cot_hbm.3, ...), custom_call_target="tpu_custom_call" | custom-call | flops 2147483648 | bytes 14680064 | tf_op jit(solution)/shard_map/remote_field/pallas_call | solution.py:485
  134.6 0.0 all-to-all-done.1.term_ref
  134.6 0.0 copy-done
  134.7 0.0 copy-done.1
  134.7 0.0 copy-start.2
  134.7 0.9 copy-done.2
  135.6 1.4 combine.1
  137.0 5.9 %all-to-all-start.2 = ((f32[8,32,128]{2,1,0:T(8,128)}), f32[8,32,128]{2,1,0:T(8,128)S(1)}, u32[]{:S(2)}, u32[]{:S(2)}) async-start(f32[8,32,128]{2,1,0:T(8,128)} %combine.1), calls=%async_computation.2 | async-start | bytes 262144 | tf_op jit(solution)/shard_map/all_to_all | solution.py:545
  142.9 2.4 %amplitudes.1 = bf16[64,16,512]{2,1,0:T(8,128)(2,1)} custom-call(f32[1040,512]{1,0:T(8,128)S(1)} %get-tuple-element.15.acc_ref, f32[1024,512]{1,0:T(8,128)} %get-tuple-element.20.field_hbm, f32[64,512]{1,0:T(8,128)} %mie_hbm.7), custom_call_target="tpu_custom_call" | custom-call | flops 524288 | bytes 5242880 | tf_op jit(solution)/shard_map/amplitudes/pallas_call | solution.py:529
  145.3 2.9 %all-to-all-done.2.in_ref = f32[8,32,128]{2,1,0:T(8,128)S(1)} async-done(((f32[8,32,128]{2,1,0:T(8,128)}), f32[8,32,128]{2,1,0:T(8,128)S(1)}, u32[]{:S(2)}, u32[]{:S(2)}) %all-to-all-start.2) | async-done | bytes 131104 | tf_op jit(solution)/shard_map/all_to_all | solution.py:545
  148.1 0.7 add_shares.1
Async XLA Ops:
  4.2 105.0 %all-to-all-start = ((bf16[32,8,16,512]{3,2,1,0:T(8,128)(2,1)}), bf16[32,8,16,512]{3,2,1,0:T(8,128)(2,1)}, u32[]{:S(2)}, u32[]{:S(2)}) async-start(bf16[32,8,16,512]{3,2,1,0:T(8,128)(2,1)} %pack_rows.1), calls=%async_computation | async-start | bytes 8388608 | tf_op jit(solution)/shard_map/all_to_all | solution.py:417
  113.6 21.0 %all-to-all-start.1 = ((bf16[32,8,512]{2,1,0:T(8,128)(2,1)}), bf16[32,8,512]{2,1,0:T(8,128)(2,1)S(1)}, u32[]{:S(2)}, u32[]{:S(2)}) async-start(bf16[32,8,512]{2,1,0:T(8,128)(2,1)} %remote_terms.1), calls=%async_computation.1 | async-start | bytes 524288 | tf_op jit(solution)/shard_map/all_to_all | solution.py:417
  122.9 11.8 %copy-start = (f32[64,512]{1,0:T(8,128)S(1)}, f32[64,512]{1,0:T(8,128)}, u32[]{:S(2)}) copy-start(f32[64,512]{1,0:T(8,128)} %mie_hbm.7) | copy-start | bytes 393220
  122.9 11.8 %copy-start.1 = (f32[256,128]{1,0:T(8,128)S(1)}, f32[256,128]{1,0:T(8,128)}, u32[]{:S(2)}) copy-start(f32[256,128]{1,0:T(8,128)} %get-tuple-element.16.owner_hbm) | copy-start | bytes 393220
  134.7 0.9 copy-start.2
  137.0 11.1 %all-to-all-start.2 = ((f32[8,32,128]{2,1,0:T(8,128)}), f32[8,32,128]{2,1,0:T(8,128)S(1)}, u32[]{:S(2)}, u32[]{:S(2)}) async-start(f32[8,32,128]{2,1,0:T(8,128)} %combine.1), calls=%async_computation.2 | async-start | bytes 262144 | tf_op jit(solution)/shard_map/all_to_all | solution.py:545

commit v4 on v3

--- a/solution.py
+++ b/solution.py
@@ -7,9 +7,11 @@
 from jax.experimental.pallas import tpu as pltpu
 from jax.sharding import PartitionSpec as P
 
-TILE = 24
+TILE = 32
 WINDOW = 3
 LANES = 128
+NEAR = 128
+SIZES = (16, 24, 32)
 PARTS = 8
 F32 = jnp.float32
 BF16 = jnp.bfloat16
@@ -33,21 +35,30 @@
 ):
     peers, cap = out_ref.shape[:2]
     part_peers = peers // PARTS
-    gets = [
-        pltpu.make_async_copy(inc_hbm, inc_ref, in_sem.at[0]),
-        pltpu.make_async_copy(mie_hbm, mie_ref, in_sem.at[1]),
-        pltpu.make_async_copy(rows_hbm, rows_ref, in_sem.at[2]),
-    ]
-    for get in gets:
-        get.start()
-    for get in gets:
-        get.wait()
-
-    def scale(p, carry):
-        start_ref[p] = (mie_ref[pl.ds(p, 1), :] * inc_ref[p].astype(F32)).astype(BF16)
-        return carry
-
-    lax.fori_loop(0, inc_ref.shape[0], scale, 0, unroll=8)
+    pieces = in_sem.shape[0] - 2
+    step = inc_ref.shape[0] // pieces
+
+    def get(piece):
+        here = pl.ds(piece * step, step)
+        return pltpu.make_async_copy(inc_hbm.at[here], inc_ref.at[here], in_sem.at[piece])
+
+    get_mie = pltpu.make_async_copy(mie_hbm, mie_ref, in_sem.at[pieces])
+    get_rows = pltpu.make_async_copy(rows_hbm, rows_ref, in_sem.at[pieces + 1])
+    get_mie.start()
+    for piece in range(pieces):
+        get(piece).start()
+    get_rows.start()
+    get_mie.wait()
+    for piece in range(pieces):
+        get(piece).wait()
+
+        def scale(i, carry, piece=piece):
+            p = piece * step + i
+            start_ref[p] = (mie_ref[pl.ds(p, 1), :] * inc_ref[p].astype(F32)).astype(BF16)
+            return carry
+
+        lax.fori_loop(0, step, scale, 0, unroll=8)
+    get_rows.wait()
 
     def put(part):
         here = pl.ds(part * part_peers, part_peers)
@@ -71,7 +82,8 @@
     mie_hbm,
     trans_hbm,
     field_ref,
-    back_ref,
+    near_ref,
+    far_hbm,
     grad_ref,
     owner_ref,
     order_ref,
@@ -85,8 +97,10 @@
     lhs_ref,
     prod_ref,
     adjoint_ref,
+    back_ref,
     in_sem,
     trans_sem,
+    far_sem,
 ):
     count_p, count_n, width = inc_ref.shape
     classes = slot_ref.shape[0]
@@ -162,6 +176,15 @@
 
     lax.fori_loop(0, classes, one_class, 0)
 
+    put_far = pltpu.make_async_copy(back_ref.at[pl.ds(NEAR, dummy - NEAR)], far_hbm, far_sem)
+    put_far.start()
+
+    def keep(i, carry):
+        near_ref[i] = back_ref[i]
+        return carry
+
+    lax.fori_loop(0, NEAR, keep, 0, unroll=4)
+
     def own(q, carry):
         lane = lax.broadcasted_iota(jnp.int32, (1, LANES), 1)
         for c in range(rows_ref.shape[0]):
@@ -178,18 +201,25 @@
         return carry
 
     lax.fori_loop(0, count_p, finish, 0, unroll=4)
-
-
-def remote_terms(arrived_hbm, back_hbm, term_ref, arrived_ref, back_ref, sem):
+    put_far.wait()
+
+
+def remote_terms(arrived_hbm, far_hbm, back_ref, term_ref, near_ref, last_ref, far_ref, sem):
     peers, cap = term_ref.shape[:2]
-    part_peers = peers // PARTS
+    rows_in = peers * cap
+    step = rows_in // PARTS
+    parts_near = NEAR // step
 
     def get(part):
-        here = pl.ds(part * part_peers * cap, part_peers * cap)
-        return (
-            pltpu.make_async_copy(arrived_hbm.at[here], arrived_ref.at[here], sem.at[0, part]),
-            pltpu.make_async_copy(back_hbm.at[here], back_ref.at[here], sem.at[1, part]),
-        )
+        start = part * step
+        here = pl.ds(start, step)
+        if part < parts_near:
+            return [pltpu.make_async_copy(arrived_hbm.at[here], near_ref.at[here], sem.at[0, part])]
+        there = pl.ds(start - NEAR, step)
+        return [
+            pltpu.make_async_copy(arrived_hbm.at[here], last_ref.at[there], sem.at[0, part]),
+            pltpu.make_async_copy(far_hbm.at[there], far_ref.at[there], sem.at[1, part]),
+        ]
 
     for part in range(PARTS):
         for copy in get(part):
@@ -197,15 +227,17 @@
     for part in range(PARTS):
         for copy in get(part):
             copy.wait()
-
-        def one(i, carry, part=part):
-            peer = part * part_peers + i
-            here = pl.ds(peer * cap, cap)
-            both = arrived_ref[here].astype(F32) * back_ref[here].astype(F32)
-            term_ref[peer] = jnp.sum(both, axis=1).astype(BF16)
+        is_near = part < parts_near
+        got_ref, kept_ref = (near_ref, back_ref) if is_near else (last_ref, far_ref)
+        base = part * step - (0 if is_near else NEAR)
+
+        def one(i, carry, part=part, got_ref=got_ref, kept_ref=kept_ref, base=base):
+            here = pl.ds(base + i * cap, cap)
+            both = got_ref[here].astype(F32) * kept_ref[here].astype(F32)
+            term_ref[part * (step // cap) + i] = jnp.sum(both, axis=1).astype(BF16)
             return carry
 
-        lax.fori_loop(0, part_peers, one, 0)
+        lax.fori_loop(0, step // cap, one, 0)
 
 
 def remote_field(
@@ -222,10 +254,8 @@
     cot_ref,
     part_ref,
     grad_ref,
-    lhs_even,
-    lhs_odd,
-    moved_even,
-    moved_odd,
+    lhs_ref,
+    moved_ref,
     in_sem,
     trans_sem,
     out_sem,
@@ -252,21 +282,19 @@
         return carry
 
     lax.fori_loop(0, count_p + 1, clear, 0, unroll=5)
-    moved_odd[...] = jnp.zeros_like(moved_odd)
     get_arrived.wait()
 
-    def gather(k, lhs, t=0):
-        base = k * stride + t * TILE
-        for i in range(TILE):
+    def tile(k, first, size):
+        base = k * stride + first
+        for i in range(size):
             source = lax.shift_right_logical(order_ref[base + i], 7)
-            lhs[pl.ds(i * count_n, count_n), :] = arrived_ref[source]
-
-    def scatter(k, moved, t=0):
-        base = k * stride + t * TILE
-        for i in range(TILE):
+            lhs_ref[pl.ds(i * count_n, count_n), :] = arrived_ref[source]
+        rows = pl.ds(0, size * count_n)
+        moved_ref[rows, :] = jnp.dot(lhs_ref[rows, :], trans_ref[k], preferred_element_type=F32)
+        for i in range(size):
             p = order_ref[base + i] & 127
             at = pl.multiple_of(p * count_n, count_n)
-            acc_ref[pl.ds(at, count_n), :] += moved[pl.ds(i * count_n, count_n), :]
+            acc_ref[pl.ds(at, count_n), :] += moved_ref[pl.ds(i * count_n, count_n), :]
 
     def fetch(k):
         get_trans(k).wait()
@@ -280,34 +308,26 @@
             for get in late:
                 get.start()
 
-    gather(0, lhs_even)
-
-    def two_classes(i, carry):
-        k = 2 * i
+    def one_class(k, carry):
         fetch(k)
-        moved_even[...] = jnp.dot(lhs_even[...], trans_ref[k], preferred_element_type=F32)
-        gather(k + 1, lhs_odd)
-        scatter(jnp.maximum(k - 1, 0), moved_odd)
-        fetch(k + 1)
-        moved_odd[...] = jnp.dot(lhs_odd[...], trans_ref[k + 1], preferred_element_type=F32)
-        gather(jnp.minimum(k + 2, classes - 1), lhs_even)
-        scatter(k, moved_even)
-        return carry
-
-    lax.fori_loop(0, classes // 2, two_classes, 0)
-    scatter(classes - 1, moved_odd)
-
-    def more(k, carry):
-        def one_tile(t, c):
-            gather(k, lhs_even, t)
-            moved_even[...] = jnp.dot(lhs_even[...], trans_ref[k], preferred_element_type=F32)
-            scatter(k, moved_even, t)
+        count = count_ref[k]
+        for low, size in zip((-1,) + SIZES, SIZES):
+            here = count > low
+            if size < TILE:
+                here = here & (count <= size)
+
+            @pl.when(here)
+            def _(size=size):
+                tile(k, 0, size)
+
+        def more(t, c):
+            tile(k, t * TILE, TILE)
             return c
 
-        lax.fori_loop(1, lax.div(count_ref[k] + (TILE - 1), TILE), one_tile, 0)
-        return carry
-
-    lax.fori_loop(0, classes, more, 0)
+        lax.fori_loop(1, lax.div(count + (TILE - 1), TILE), more, 0)
+        return carry
+
+    lax.fori_loop(0, classes, one_class, 0)
     for get in late:
         get.wait()
 
@@ -400,6 +420,10 @@
     return pltpu.with_memory_space_constraint(x, pltpu.VMEM)
 
 
+def far_off(x):
+    return pltpu.with_memory_space_constraint(x, pltpu.HBM)
+
+
 def body(incident, cotangent, mie, trans, send_rows, partner_slot):
     count_p, count_n, width = incident.shape
     classes = trans.shape[0]
@@ -427,7 +451,7 @@
             pltpu.VMEM((count_p, count_n, width), BF16),
             pltpu.VMEM((count_p, count_n, width), BF16),
             pltpu.VMEM((peers, cap, count_n, width), BF16),
-            pltpu.SemaphoreType.DMA((3,)),
+            pltpu.SemaphoreType.DMA((6,)),
             pltpu.SemaphoreType.DMA((PARTS,)),
         ],
         compiler_params=params(),
@@ -436,18 +460,20 @@
     )(rows, mie, incident)
     arrived = send(packed).reshape(remote_rows, count_n, width)
 
-    field, back, part, owner, order, count = pl.pallas_call(
+    far_rows = remote_rows - NEAR
+    field, near, far, part, owner, order, count = pl.pallas_call(
         local_part,
         out_shape=(
             jax.ShapeDtypeStruct((total, width), F32),
-            jax.ShapeDtypeStruct((remote_rows + 1, count_n, width), BF16),
+            pltpu.VMEM((NEAR, count_n, width), BF16),
+            jax.ShapeDtypeStruct((far_rows, count_n, width), BF16),
             jax.ShapeDtypeStruct((count_p, width), F32),
             jax.ShapeDtypeStruct((remote_rows, LANES), F32),
             jax.ShapeDtypeStruct((classes * (count_p + TILE),), jnp.int32),
             jax.ShapeDtypeStruct((classes,), jnp.int32),
         ),
         in_specs=[smem(), smem()] + [hbm()] * 4,
-        out_specs=(vmem(),) * 4 + (smem(),) * 2,
+        out_specs=(vmem(), vmem(), hbm(), vmem(), vmem(), smem(), smem()),
         scratch_shapes=[
             pltpu.VMEM((count_p, count_n, width), BF16),
             pltpu.VMEM((count_p, count_n, width), BF16),
@@ -458,28 +484,32 @@
             pltpu.VMEM((total, width), BF16),
             pltpu.VMEM((total, width), F32),
             pltpu.VMEM((count_p + 1, count_n, width), F32),
+            pltpu.VMEM((remote_rows + 1, count_n, width), BF16),
             pltpu.SemaphoreType.DMA((3,)),
             pltpu.SemaphoreType.DMA((classes,)),
+            pltpu.SemaphoreType.DMA,
         ],
         compiler_params=params(),
         cost_estimate=cost(4 * classes * row_ops * width, 16),
         name="local_part",
     )(slots, rows, incident, cotangent, mie, trans)
+    near = stay(near)
 
     term = pl.pallas_call(
         remote_terms,
         out_shape=jax.ShapeDtypeStruct((peers, cap, width), BF16),
-        in_specs=[hbm(), hbm()],
+        in_specs=[hbm(), hbm(), vmem()],
         out_specs=vmem(),
         scratch_shapes=[
-            pltpu.VMEM((remote_rows, count_n, width), BF16),
-            pltpu.VMEM((remote_rows, count_n, width), BF16),
+            pltpu.VMEM((NEAR, count_n, width), BF16),
+            pltpu.VMEM((far_rows, count_n, width), BF16),
+            pltpu.VMEM((far_rows, count_n, width), BF16),
             pltpu.SemaphoreType.DMA((2, PARTS)),
         ],
-        compiler_params=params(),
+        compiler_params=params(58),
         cost_estimate=cost(4 * row_ops, 8),
         name="remote_terms",
-    )(arrived, back)
+    )(arrived, far, near)
     term = send(term)
 
     acc, part = pl.pallas_call(
@@ -497,8 +527,6 @@
             pltpu.VMEM((count_p, width), F32),
             pltpu.VMEM((count_p, width), F32),
             pltpu.VMEM((TILE * count_n, width), BF16),
-            pltpu.VMEM((TILE * count_n, width), BF16),
-            pltpu.VMEM((TILE * count_n, width), F32),
             pltpu.VMEM((TILE * count_n, width), F32),
             pltpu.SemaphoreType.DMA((3,)),
             pltpu.SemaphoreType.DMA((classes,)),
@@ -524,7 +552,7 @@
         compiler_params=params(24),
         cost_estimate=cost(row_ops, 1),
         name="combine",
-    )(owner, mie, part, term)
+    )(far_off(owner), far_off(mie), far_off(part), term)
     mine, field = lax.optimization_barrier((mine, field))
     amplitude = pl.pallas_call(
         amplitudes,

time: 149 us -> 149 us (level)
  Pallas kernels: 60.5 us -> 58 us
  starting transfers between devices: 27.3 us -> 28.9 us
    all_to_all x1, starting transfers between devices: 5.86 us -> 7.51 us  [body(): lax.all_to_all(mine, 'dir', split_axis=0, concat_axis=0, tiled=True)]
    pallas_call x1, Pallas kernels: 11.7 us -> 10.1 us  [body(): pl.pallas_call(remote_field, out_shape=(pltpu.VMEM((total + count_n, widt...]
  transfers between devices with their start and end apart: 3 -> 3, of which waited for: 2 -> 2; matrix products, arithmetic and copies ran while one was open for 0% -> 0% of each run, Pallas kernels for 34% -> 32%
where the time goes in v4:
time: 149 us; the launch traced here: 148 us
  waiting for transfers between devices  60.5 us (41%)
  Pallas kernels  58 us (39%)
  starting transfers between devices  28.9 us (19%)
    all_to_all x2, waiting for transfers between devices, send(): return lax.all_to_all(x, 'dom', split_axis=0, concat_axis=0, tiled=True)  57.6 us
    pallas_call x1, Pallas kernels, body(): pl.pallas_call(local_part, out_shape=(jax.ShapeDtypeStruct((total, width)...  35.2 us
    all_to_all x2, starting transfers between devices, send(): return lax.all_to_all(x, 'dom', split_axis=0, concat_axis=0, tiled=True)  21.4 us
    pallas_call x1, Pallas kernels, body(): pl.pallas_call(remote_field, out_shape=(pltpu.VMEM((total + count_n, widt...  10.1 us
    all_to_all x1, starting transfers between devices, body(): lax.all_to_all(mine, 'dir', split_axis=0, concat_axis=0, tiled=True)  7.51 us
    pallas_call x1, Pallas kernels, body(): pl.pallas_call(remote_terms, out_shape=jax.ShapeDtypeStruct((peers, cap,...  4.21 us
    pallas_call x1, Pallas kernels, body(): pl.pallas_call(pack_rows, out_shape=jax.ShapeDtypeStruct((peers, cap, cou...  3.46 us
  transfers between devices with their start and end apart: 3, of which 2 were waited for; matrix products, arithmetic and copies ran while one was open for 0% of the time, Pallas kernels for 32%

profile of v4, /device:TPU:1, one launch (start us, length us, event | category | flops | bytes accessed | tf_op | source)
XLA Modules:
  0.0 148.1 jit_solution(16321348039127148025)
XLA Ops:
  0.6 3.5 %pack_rows.1 = bf16[32,8,16,512]{3,2,1,0:T(8,128)(2,1)} custom-call(s32[8,32]{1,0:T(8,128)} %bitcast.5, f32[64,512]{1,0:T(8,128)} %mie_hbm.7, bf16[64,16,512]{2,1,0:T(8,128)(2,1)} %inc_hbm.3), custom_call_target="tpu_custom_call" | custom-call | flops 524288 | bytes 4194304 | tf_op jit(solution)/shard_map/pack_rows/pallas_call | solution.py:443
  4.1 12.2 %all-to-all-start = ((bf16[32,8,16,512]{3,2,1,0:T(8,128)(2,1)}), bf16[32,8,16,512]{3,2,1,0:T(8,128)(2,1)}, u32[]{:S(2)}, u32[]{:S(2)}) async-start(bf16[32,8,16,512]{3,2,1,0:T(8,128)(2,1)} %pack_rows.1), calls=%async_computation | async-start | bytes 8388608 | tf_op jit(solution)/shard_map/all_to_all | solution.py:441
  16.3 35.2 %local_part.1 = (f32[1024,512]{1,0:T(8,128)}, bf16[128,16,512]{2,1,0:T(8,128)(2,1)S(1)}, bf16[128,16,512]{2,1,0:T(8,128)(2,1)}, f32[64,512]{1,0:T(8,128)}, f32[2...) custom-call(s32[12,64]{1,0:T(8,128)} %bitcast.7, s32[8,32]{1,0:T(8,128)} %bitcast.6, bf16[64,16,512]{2,1,0:T(8,128)(2,1)} %inc_hbm.3, ...), custom_call_target="tpu_custom_call" | custom-call | flops 12884901888 | bytes 16777216 | tf_op jit(solution)/shard_map/local_part/pallas_call | solution.py:464
  51.5 57.6 %all-to-all-done = bf16[32,8,16,512]{3,2,1,0:T(8,128)(2,1)} async-done(((bf16[32,8,16,512]{3,2,1,0:T(8,128)(2,1)}), bf16[32,8,16,512]{3,2,1,0:T(8,128)(2,1)}, u32[]{:S(2)}, u32[]{:S(2)}) %all-to-all-start) | async-done | bytes 4194336 | tf_op jit(solution)/shard_map/all_to_all | solution.py:441
  109.1 4.2 %remote_terms.1 = bf16[32,8,512]{2,1,0:T(8,128)(2,1)} custom-call(bf16[256,16,512]{2,1,0:T(8,128)(2,1)} %bitcast.4.arrived_hbm, bf16[128,16,512]{2,1,0:T(8,128)(2,1)} %get-tuple-element.19.far_hbm, bf16[128,16,512]{2,1,0:T(8,128)(2,1)S(1)} %get-tuple-element.20.back_ref), custom_call_target="tpu_custom_call" | custom-call | flops 2097152 | bytes 8388608 | tf_op jit(solution)/shard_map/remote_terms/pallas_call | solution.py:498
  113.3 9.2 %all-to-all-start.1 = ((bf16[32,8,512]{2,1,0:T(8,128)(2,1)}), bf16[32,8,512]{2,1,0:T(8,128)(2,1)S(1)}, u32[]{:S(2)}, u32[]{:S(2)}) async-start(bf16[32,8,512]{2,1,0:T(8,128)(2,1)} %remote_terms.1), calls=%async_computation.1 | async-start | bytes 524288 | tf_op jit(solution)/shard_map/all_to_all | solution.py:441
  122.5 10.1 %remote_field.1 = (f32[1040,512]{1,0:T(8,128)S(1)}, f32[64,512]{1,0:T(8,128)}) custom-call(s32[1152]{0:T(1024)} %get-tuple-element.13.order_ref, s32[12]{0:T(128)} %get-tuple-element.14.count_ref, bf16[256,16,512]{2,1,0:T(8,128)(2,1)} %bitcast.4.arrived_hbm, bf16[12,512,512]{2,1,0:T(8,128)(2,1)} %trans_hbm.3, bf16[64,16,512]{2,1,0:T(8,128)(2,1)} %cot_hbm.3, ...), custom_call_target="tpu_custom_call" | custom-call | flops 2147483648 | bytes 14680064 | tf_op jit(solution)/shard_map/remote_field/pallas_call | solution.py:515
  132.6 0.0 all-to-all-done.1.term_ref
  132.6 2.0 %combine.1 = f32[8,32,128]{2,1,0:T(8,128)} custom-call(f32[256,128]{1,0:T(8,128)} %get-tuple-element.17.owner_hbm, f32[64,512]{1,0:T(8,128)} %mie_hbm.7, f32[64,512]{1,0:T(8,128)} %get-tuple-element.18.part_hbm, bf16[32,8,512]{2,1,0:T(8,128)(2,1)S(1)} %all-to-all-done.1.term_ref), custom_call_target="tpu_custom_call" | custom-call | flops 524288 | bytes 1048576 | tf_op jit(solution)/shard_map/combine/pallas_call | solution.py:541
  134.6 7.5 %all-to-all-start.2 = ((f32[8,32,128]{2,1,0:T(8,128)}), f32[8,32,128]{2,1,0:T(8,128)S(1)}, u32[]{:S(2)}, u32[]{:S(2)}) async-start(f32[8,32,128]{2,1,0:T(8,128)} %combine.1), calls=%async_computation.2 | async-start | bytes 262144 | tf_op jit(solution)/shard_map/all_to_all | solution.py:573
  142.2 2.4 %amplitudes.1 = bf16[64,16,512]{2,1,0:T(8,128)(2,1)} custom-call(f32[1040,512]{1,0:T(8,128)S(1)} %get-tuple-element.16.acc_ref, f32[1024,512]{1,0:T(8,128)} %get-tuple-element.22.field_hbm, f32[64,512]{1,0:T(8,128)} %mie_hbm.7), custom_call_target="tpu_custom_call" | custom-call | flops 524288 | bytes 5242880 | tf_op jit(solution)/shard_map/amplitudes/pallas_call | solution.py:557
  144.6 2.9 %all-to-all-done.2.in_ref = f32[8,32,128]{2,1,0:T(8,128)S(1)} async-done(((f32[8,32,128]{2,1,0:T(8,128)}), f32[8,32,128]{2,1,0:T(8,128)S(1)}, u32[]{:S(2)}, u32[]{:S(2)}) %all-to-all-start.2) | async-done | bytes 131104 | tf_op jit(solution)/shard_map/all_to_all | solution.py:573
  147.4 0.7 add_shares.1
Async XLA Ops:
  4.1 105.0 %all-to-all-start = ((bf16[32,8,16,512]{3,2,1,0:T(8,128)(2,1)}), bf16[32,8,16,512]{3,2,1,0:T(8,128)(2,1)}, u32[]{:S(2)}, u32[]{:S(2)}) async-start(bf16[32,8,16,512]{3,2,1,0:T(8,128)(2,1)} %pack_rows.1), calls=%async_computation | async-start | bytes 8388608 | tf_op jit(solution)/shard_map/all_to_all | solution.py:441
  113.3 19.3 %all-to-all-start.1 = ((bf16[32,8,512]{2,1,0:T(8,128)(2,1)}), bf16[32,8,512]{2,1,0:T(8,128)(2,1)S(1)}, u32[]{:S(2)}, u32[]{:S(2)}) async-start(bf16[32,8,512]{2,1,0:T(8,128)(2,1)} %remote_terms.1), calls=%async_computation.1 | async-start | bytes 524288 | tf_op jit(solution)/shard_map/all_to_all | solution.py:441
  134.6 12.8 %all-to-all-start.2 = ((f32[8,32,128]{2,1,0:T(8,128)}), f32[8,32,128]{2,1,0:T(8,128)S(1)}, u32[]{:S(2)}, u32[]{:S(2)}) async-start(f32[8,32,128]{2,1,0:T(8,128)} %combine.1), calls=%async_computation.2 | async-start | bytes 262144 | tf_op jit(solution)/shard_map/all_to_all | solution.py:573

commit v5 on v4

--- a/solution.py
+++ b/solution.py
@@ -241,24 +241,29 @@
 
 
 def remote_field(
+    scale,
     order_ref,
     count_ref,
     arrived_hbm,
     trans_hbm,
     cot_hbm,
     part_hbm,
+    mie_hbm,
+    owner_hbm,
     acc_ref,
-    grad_hbm,
+    grad_ref,
+    weight_ref,
+    owner_ref,
     arrived_ref,
     trans_ref,
     cot_ref,
     part_ref,
-    grad_ref,
+    mie_ref,
+    slots_ref,
     lhs_ref,
     moved_ref,
     in_sem,
     trans_sem,
-    out_sem,
 ):
     classes = trans_ref.shape[0]
     count_p, count_n, width = cot_ref.shape
@@ -267,6 +272,8 @@
     late = [
         pltpu.make_async_copy(cot_hbm, cot_ref, in_sem.at[1]),
         pltpu.make_async_copy(part_hbm, part_ref, in_sem.at[2]),
+        pltpu.make_async_copy(mie_hbm, mie_ref, in_sem.at[3]),
+        pltpu.make_async_copy(owner_hbm, slots_ref, in_sem.at[4]),
     ]
 
     def get_trans(k):
@@ -331,17 +338,17 @@
     for get in late:
         get.wait()
 
+    weight_ref[...] = scale / mie_ref[...]
+    owner_ref[...] = jnp.transpose(slots_ref[...]).astype(BF16)
+
     def finish(p, carry):
         at = pl.multiple_of(p * count_n, count_n)
-        grad_ref[pl.ds(p, 1), :] = part_ref[pl.ds(p, 1), :] + jnp.sum(
-            cot_ref[p].astype(F32) * acc_ref[pl.ds(at, count_n), :], axis=0, keepdims=True
-        )
+        both = cot_ref[p].astype(F32) * acc_ref[pl.ds(at, count_n), :]
+        summed = part_ref[pl.ds(p, 1), :] + jnp.sum(both, axis=0, keepdims=True)
+        grad_ref[pl.ds(p, 1), :] = summed * scale
         return carry
 
     lax.fori_loop(0, count_p, finish, 0, unroll=4)
-    put = pltpu.make_async_copy(grad_ref, grad_hbm, out_sem)
-    put.start()
-    put.wait()
 
 
 def amplitudes(acc_ref, field_hbm, mie_hbm, amp_hbm, field_ref, mie_ref, amp_ref, in_sem, out_sem):
@@ -377,24 +384,14 @@
         put(part).wait()
 
 
-def combine(scale, owner_hbm, mie_hbm, part_hbm, term_ref, out_ref, owner_ref, mie_ref, part_ref, sem):
-    gets = [
-        pltpu.make_async_copy(owner_hbm, owner_ref, sem.at[0]),
-        pltpu.make_async_copy(mie_hbm, mie_ref, sem.at[1]),
-        pltpu.make_async_copy(part_hbm, part_ref, sem.at[2]),
-    ]
-    for get in gets:
-        get.start()
-    for get in gets:
-        get.wait()
-    count_p, width = mie_ref.shape
-    mine = lax.dot_general(
-        owner_ref[...].astype(BF16),
-        term_ref[...].reshape(owner_ref.shape[0], width),
-        (((0,), (0,)), ((), ())),
+def combine(owner_ref, weight_ref, part_ref, term_ref, out_ref):
+    count_p, width = weight_ref.shape
+    mine = jnp.dot(
+        owner_ref[...],
+        term_ref[...].reshape(owner_ref.shape[1], width),
         preferred_element_type=F32,
     )
-    whole = (part_ref[...] + mine[:count_p] / mie_ref[...]) * scale
+    whole = part_ref[...] + mine[:count_p] * weight_ref[...]
     dirs, half, pair = out_ref.shape
     share = pair // 2
     for r in range(dirs):
@@ -418,10 +415,6 @@
 
 def stay(x):
     return pltpu.with_memory_space_constraint(x, pltpu.VMEM)
-
-
-def far_off(x):
-    return pltpu.with_memory_space_constraint(x, pltpu.HBM)
 
 
 def body(incident, cotangent, mie, trans, send_rows, partner_slot):
@@ -512,47 +505,43 @@
     )(arrived, far, near)
     term = send(term)
 
-    acc, part = pl.pallas_call(
-        remote_field,
+    acc, part, weight, owner_near = pl.pallas_call(
+        functools.partial(remote_field, 1.0 / (count_n * dirs)),
         out_shape=(
             pltpu.VMEM((total + count_n, width), F32),
-            jax.ShapeDtypeStruct((count_p, width), F32),
+            pltpu.VMEM((count_p, width), F32),
+            pltpu.VMEM((count_p, width), F32),
+            pltpu.VMEM((LANES, remote_rows), BF16),
         ),
-        in_specs=[smem(), smem()] + [hbm()] * 4,
-        out_specs=(vmem(), hbm()),
+        in_specs=[smem(), smem()] + [hbm()] * 6,
+        out_specs=(vmem(),) * 4,
         scratch_shapes=[
             pltpu.VMEM((remote_rows, count_n, width), BF16),
             pltpu.VMEM((classes, width, width), BF16),
             pltpu.VMEM((count_p, count_n, width), BF16),
             pltpu.VMEM((count_p, width), F32),
             pltpu.VMEM((count_p, width), F32),
+            pltpu.VMEM((remote_rows, LANES), F32),
             pltpu.VMEM((TILE * count_n, width), BF16),
             pltpu.VMEM((TILE * count_n, width), F32),
-            pltpu.SemaphoreType.DMA((3,)),
+            pltpu.SemaphoreType.DMA((5,)),
             pltpu.SemaphoreType.DMA((classes,)),
-            pltpu.SemaphoreType.DMA,
         ],
         compiler_params=params(56),
         cost_estimate=cost(2 * remote_rows * count_n * width * width, 14),
         name="remote_field",
-    )(order, count, arrived, trans, cotangent, part)
-    acc = stay(acc)
+    )(order, count, arrived, trans, cotangent, part, mie, owner)
+    acc, part, weight, owner_near = (stay(x) for x in (acc, part, weight, owner_near))
 
     mine = pl.pallas_call(
-        functools.partial(combine, 1.0 / (count_n * dirs)),
+        combine,
         out_shape=jax.ShapeDtypeStruct((dirs, count_p // 2, 2 * width // dirs), F32),
-        in_specs=[hbm()] * 3 + [vmem()],
+        in_specs=[vmem()] * 4,
         out_specs=vmem(),
-        scratch_shapes=[
-            pltpu.VMEM((remote_rows, LANES), F32),
-            pltpu.VMEM((count_p, width), F32),
-            pltpu.VMEM((count_p, width), F32),
-            pltpu.SemaphoreType.DMA((3,)),
-        ],
         compiler_params=params(24),
         cost_estimate=cost(row_ops, 1),
         name="combine",
-    )(far_off(owner), far_off(mie), far_off(part), term)
+    )(owner_near, weight, part, term)
     mine, field = lax.optimization_barrier((mine, field))
     amplitude = pl.pallas_call(
         amplitudes,

time: 149 us -> 148 us (level)
  Pallas kernels: 58 us -> 56.3 us
    pallas_call x2, Pallas kernels: 12.1 us -> 10.4 us  [the longest x1 9.46 us: body(): pl.pallas_call(functools.partial(remote_field, 1.0 / (count_n * dirs)), o...]
  transfers between devices with their start and end apart: 3 -> 3, of which waited for: 2 -> 3; matrix products, arithmetic and copies ran while one was open for 0% -> 0% of each run, Pallas kernels for 32% -> 32%
where the time goes in v5:
time: 148 us; the launch traced here: 147 us
  waiting for transfers between devices  60.7 us (41%)
  Pallas kernels  56.3 us (38%)
  starting transfers between devices  29.3 us (20%)
    all_to_all x2, waiting for transfers between devices, send(): return lax.all_to_all(x, 'dom', split_axis=0, concat_axis=0, tiled=True)  57.8 us
    pallas_call x1, Pallas kernels, body(): pl.pallas_call(local_part, out_shape=(jax.ShapeDtypeStruct((total, width)...  35.2 us
    all_to_all x2, starting transfers between devices, send(): return lax.all_to_all(x, 'dom', split_axis=0, concat_axis=0, tiled=True)  21.4 us
    pallas_call x1, Pallas kernels, body(): pl.pallas_call(functools.partial(remote_field, 1.0 / (count_n * dirs)), o...  9.46 us
    all_to_all x1, starting transfers between devices, body(): lax.all_to_all(mine, 'dir', split_axis=0, concat_axis=0, tiled=True)  7.94 us
    pallas_call x1, Pallas kernels, body(): pl.pallas_call(remote_terms, out_shape=jax.ShapeDtypeStruct((peers, cap,...  4.21 us
    pallas_call x1, Pallas kernels, body(): pl.pallas_call(pack_rows, out_shape=jax.ShapeDtypeStruct((peers, cap, cou...  3.46 us
  transfers between devices with their start and end apart: 3, of which 3 were waited for; matrix products, arithmetic and copies ran while one was open for 0% of the time, Pallas kernels for 32%

profile of v5, /device:TPU:1, one launch (start us, length us, event | category | flops | bytes accessed | tf_op | source)
XLA Modules:
  0.0 147.0 jit_solution(14787391044070645212)
XLA Ops:
  0.6 3.5 %pack_rows.1 = bf16[32,8,16,512]{3,2,1,0:T(8,128)(2,1)} custom-call(s32[8,32]{1,0:T(8,128)} %bitcast.5, f32[64,512]{1,0:T(8,128)} %mie_hbm.7, bf16[64,16,512]{2,1,0:T(8,128)(2,1)} %inc_hbm.3), custom_call_target="tpu_custom_call" | custom-call | flops 524288 | bytes 4194304 | tf_op jit(solution)/shard_map/pack_rows/pallas_call | solution.py:436
  4.1 12.2 %all-to-all-start = ((bf16[32,8,16,512]{3,2,1,0:T(8,128)(2,1)}), bf16[32,8,16,512]{3,2,1,0:T(8,128)(2,1)}, u32[]{:S(2)}, u32[]{:S(2)}) async-start(bf16[32,8,16,512]{3,2,1,0:T(8,128)(2,1)} %pack_rows.1), calls=%async_computation | async-start | bytes 8388608 | tf_op jit(solution)/shard_map/all_to_all | solution.py:434
  16.3 35.2 %local_part.1 = (f32[1024,512]{1,0:T(8,128)}, bf16[128,16,512]{2,1,0:T(8,128)(2,1)S(1)}, bf16[128,16,512]{2,1,0:T(8,128)(2,1)}, f32[64,512]{1,0:T(8,128)}, f32[2...) custom-call(s32[12,64]{1,0:T(8,128)} %bitcast.7, s32[8,32]{1,0:T(8,128)} %bitcast.6, bf16[64,16,512]{2,1,0:T(8,128)(2,1)} %inc_hbm.3, ...), custom_call_target="tpu_custom_call" | custom-call | flops 12884901888 | bytes 16777216 | tf_op jit(solution)/shard_map/local_part/pallas_call | solution.py:457
  51.5 57.6 %all-to-all-done = bf16[32,8,16,512]{3,2,1,0:T(8,128)(2,1)} async-done(((bf16[32,8,16,512]{3,2,1,0:T(8,128)(2,1)}), bf16[32,8,16,512]{3,2,1,0:T(8,128)(2,1)}, u32[]{:S(2)}, u32[]{:S(2)}) %all-to-all-start) | async-done | bytes 4194336 | tf_op jit(solution)/shard_map/all_to_all | solution.py:434
  109.1 4.2 %remote_terms.1 = bf16[32,8,512]{2,1,0:T(8,128)(2,1)} custom-call(bf16[256,16,512]{2,1,0:T(8,128)(2,1)} %bitcast.4.arrived_hbm, bf16[128,16,512]{2,1,0:T(8,128)(2,1)} %get-tuple-element.23.far_hbm, bf16[128,16,512]{2,1,0:T(8,128)(2,1)S(1)} %get-tuple-element.24.back_ref), custom_call_target="tpu_custom_call" | custom-call | flops 2097152 | bytes 8388608 | tf_op jit(solution)/shard_map/remote_terms/pallas_call | solution.py:491
  113.3 9.2 %all-to-all-start.1 = ((bf16[32,8,512]{2,1,0:T(8,128)(2,1)}), bf16[32,8,512]{2,1,0:T(8,128)(2,1)S(1)}, u32[]{:S(2)}, u32[]{:S(2)}) async-start(bf16[32,8,512]{2,1,0:T(8,128)(2,1)} %remote_terms.1), calls=%async_computation.1 | async-start | bytes 524288 | tf_op jit(solution)/shard_map/all_to_all | solution.py:434
  122.5 9.5 %remote_field.1 = (f32[1040,512]{1,0:T(8,128)S(1)}, f32[64,512]{1,0:T(8,128)S(1)}, f32[64,512]{1,0:T(8,128)S(1)}, bf16[128,256]{1,0:T(8,128)(2,1)S(1)}) custom-call(s32[1152]{0:T(1024)} %get-tuple-element.15.order_ref, s32[12]{0:T(128)} %get-tuple-element.16.count_ref, bf16[256,16,512]{2,1,0:T(8,128)(2,1)} %bitcast.4.arrived_hbm, ...), custom_call_target="tpu_custom_call" | custom-call | flops 2147483648 | bytes 14680064 | tf_op jit(solution)/shard_map/remote_field/pallas_call | solution.py:508
  132.0 0.2 all-to-all-done.1.term_ref
  132.2 0.9 combine.1
  133.1 7.9 %all-to-all-start.2 = ((f32[8,32,128]{2,1,0:T(8,128)}), f32[8,32,128]{2,1,0:T(8,128)S(1)}, u32[]{:S(2)}, u32[]{:S(2)}) async-start(f32[8,32,128]{2,1,0:T(8,128)} %combine.1), calls=%async_computation.2 | async-start | bytes 262144 | tf_op jit(solution)/shard_map/all_to_all | solution.py:562
  141.1 2.4 %amplitudes.1 = bf16[64,16,512]{2,1,0:T(8,128)(2,1)} custom-call(f32[1040,512]{1,0:T(8,128)S(1)} %get-tuple-element.19.acc_ref, f32[1024,512]{1,0:T(8,128)} %get-tuple-element.26.field_hbm, f32[64,512]{1,0:T(8,128)} %mie_hbm.7), custom_call_target="tpu_custom_call" | custom-call | flops 524288 | bytes 5242880 | tf_op jit(solution)/shard_map/amplitudes/pallas_call | solution.py:546
  143.5 2.9 %all-to-all-done.2.in_ref = f32[8,32,128]{2,1,0:T(8,128)S(1)} async-done(((f32[8,32,128]{2,1,0:T(8,128)}), f32[8,32,128]{2,1,0:T(8,128)S(1)}, u32[]{:S(2)}, u32[]{:S(2)}) %all-to-all-start.2) | async-done | bytes 131104 | tf_op jit(solution)/shard_map/all_to_all | solution.py:562
  146.3 0.7 add_shares.1
Async XLA Ops:
  4.1 105.0 %all-to-all-start = ((bf16[32,8,16,512]{3,2,1,0:T(8,128)(2,1)}), bf16[32,8,16,512]{3,2,1,0:T(8,128)(2,1)}, u32[]{:S(2)}, u32[]{:S(2)}) async-start(bf16[32,8,16,512]{3,2,1,0:T(8,128)(2,1)} %pack_rows.1), calls=%async_computation | async-start | bytes 8388608 | tf_op jit(solution)/shard_map/all_to_all | solution.py:434
  113.3 18.9 %all-to-all-start.1 = ((bf16[32,8,512]{2,1,0:T(8,128)(2,1)}), bf16[32,8,512]{2,1,0:T(8,128)(2,1)S(1)}, u32[]{:S(2)}, u32[]{:S(2)}) async-start(bf16[32,8,512]{2,1,0:T(8,128)(2,1)} %remote_terms.1), calls=%async_computation.1 | async-start | bytes 524288 | tf_op jit(solution)/shard_map/all_to_all | solution.py:434
  133.1 13.2 %all-to-all-start.2 = ((f32[8,32,128]{2,1,0:T(8,128)}), f32[8,32,128]{2,1,0:T(8,128)S(1)}, u32[]{:S(2)}, u32[]{:S(2)}) async-start(f32[8,32,128]{2,1,0:T(8,128)} %combine.1), calls=%async_computation.2 | async-start | bytes 262144 | tf_op jit(solution)/shard_map/all_to_all | solution.py:562
